TPU v7x, 512 devices: a whole 4x8x8 slice. The times are simulated.
512 devices in a mesh: layer: 8 (over x, z_hi), ex: 16 (over y, core), width: 4 (over z_lo).
Axes of the slice: x: 4, y: 8, z: 8 (z_hi: 2, z_lo: 4; z = z_hi * 4 + z_lo), core: 2. Of those that a mesh axis runs over, the one named last changes fastest.
Arguments:
- activations: bfloat16 [8, 128, 32, 8192], P('layer', 'ex', None, 'width'), may hold values from -6 to 6
- gradients: bfloat16 [8, 128, 32, 28672], P('layer', 'ex', None, 'width'), may hold values from -6 to 6
- act_scale: float32 [8, 8192], P('layer', 'width'), may hold values from 0.25 to 4
- grad_scale: float32 [8, 28672], P('layer', 'width'), may hold values from 0.25 to 4
- counts: int32 [128], P('ex'), may hold values from 1 to 32, 3072 in all
- loss_mask: int32 [128, 32], P('ex'), may hold values 0 or 1
Outputs:
- influence: float32 [3, 128, 8], P(None, 'ex', 'layer')
Inputs may be any that keep to these rules, and one draw needn't show every extreme that they name: counts[e] is the number of filled token slots of example e; the largest is reached in every draw.
All inputs are finite; a program needn't handle non-finite values. No bound on the sum of `counts` or of `loss_mask` on one device may be relied on, other than what follows from the above.
Results may differ from a plain program's by a relative error of at most 0.004.
Values may be sent and summed in bfloat16 or wider, within the bound.
No kernel may reach another device: no remote copies, remote signals or barrier semaphores. Data moves between devices by JAX's collectives and lax.ppermute only.
A program may use at most 64 MiB of HBM per device.

v0:
```python
import math

import jax
import jax.numpy as jnp
from jax import lax
from jax.sharding import PartitionSpec as P

D = 8192
FF = 28672
HOPS = 2


def from_behind(value, axis, steps):
    count = lax.axis_size(axis)
    pairs = [(source, (source + steps) % count) for source in range(count)]
    return lax.ppermute(value, axis, pairs)


def local(activations, gradients, act_scale, grad_scale, counts, loss_mask):
    ex_local, tok_slots = loss_mask.shape
    row_count = ex_local * tok_slots
    own_acts = activations[0].reshape(row_count, -1)
    own_grads = gradients[0].reshape(row_count, -1)
    positions = lax.broadcasted_iota(jnp.int32, (ex_local, tok_slots), 1)
    token_weight = (positions < counts[:, None]).astype(jnp.int32) * loss_mask
    weight_rows = token_weight.astype(jnp.float32).reshape(row_count)
    stat_acts = (own_acts.astype(jnp.float32) * act_scale[0]).astype(jnp.bfloat16)
    stat_grads = (own_grads.astype(jnp.float32) * grad_scale[0]).astype(jnp.bfloat16)
    factor = 1.0 / (math.sqrt(D * FF) * tok_slots)
    contract = (((1,), (1,)), ((), ()))

    def pair_scores(partner):
        move_acts, move_grads, move_weight = partner
        act_gram = lax.dot_general(
            stat_acts, move_acts, contract, preferred_element_type=jnp.float32
        )
        grad_gram = lax.dot_general(
            stat_grads, move_grads, contract, preferred_element_type=jnp.float32
        )
        act_gram, grad_gram = lax.psum((act_gram, grad_gram), "width")
        product = (
            act_gram * grad_gram * weight_rows[:, None] * move_weight.astype(jnp.float32)[None, :]
        )
        return product.reshape(ex_local, tok_slots, ex_local, tok_slots).sum(axis=(1, 3)) * factor

    travel = (own_acts, own_grads, weight_rows.astype(jnp.bfloat16))
    scores = [pair_scores(travel)]
    partner = travel
    for distance in range(HOPS):
        partner = from_behind((partner[0], partner[1], partner[2]), "ex", 1)
        scores.append(pair_scores(partner))
    local_ex = lax.broadcasted_iota(jnp.int32, (ex_local, ex_local), 0)
    column_ex = lax.broadcasted_iota(jnp.int32, (ex_local, ex_local), 1)
    not_self = (local_ex != column_ex).astype(jnp.float32)
    scores[0] = scores[0] * not_self
    stacked = jnp.stack(scores)
    summed = lax.psum_scatter(stacked, "layer", scatter_dimension=2, tiled=True)
    return summed


def solution(mesh):
    in_specs = (
        P("layer", "ex", None, "width"),
        P("layer", "ex", None, "width"),
        P("layer", "width"),
        P("layer", "width"),
        P("ex"),
        P("ex", None),
    )
    out_specs = P(None, "ex", "layer")
    return jax.shard_map(local, mesh=mesh, in_specs=in_specs, out_specs=out_specs, check_vma=False)
```

profile of v0, /device:TPU:8, one launch (start us, length us, event | category | flops | bytes accessed | tf_op | source)
XLA Modules:
  0.0 273.5 jit_solution(723164037195865327)
XLA Ops:
  6.5 0.0 collective-permute-start.1
  6.5 1.7 collective-permute-start
  8.2 40.8 %collective-permute-done.1 = bf16[256,7168]{1,0:T(8,128)(2,1)S(1)} collective-permute-done((bf16[256,7168]{1,0:T(8,128)(2,1)}, bf16[256,7168]{1,0:T(8,128)(2,1)S(1)}, u32[]{:S(2)}, u32[]{:S(2)}) %collective-permute-start.1) | collective-permute-done | bytes 3670048 | tf_op jit(solution)/shard_map/ppermute | solution.py:16
  49.1 3.0 %multiply_convert_fusion.1 = bf16[1,8,32,7168]{3,2,1,0:T(8,128)(2,1)S(1)} fusion(bf16[1,8,32,7168]{3,2,1,0:T(8,128)(2,1)} %param.7, f32[7168]{0:T(1024)} %bitcast.31), kind=kLoop, calls=%fused_computation.1 | loop fusion | flops 5505024 | bytes 7368704 | tf_op jit(solution)/shard_map/convert_element_type | solution.py:28
  52.0 0.0 copy-start.1
  52.1 0.2 multiply_convert_fusion.5
  52.3 8.0 %collective-permute-done = bf16[256,2048]{1,0:T(8,128)(2,1)S(1)} collective-permute-done((bf16[256,2048]{1,0:T(8,128)(2,1)}, bf16[256,2048]{1,0:T(8,128)(2,1)S(1)}, u32[]{:S(2)}, u32[]{:S(2)}) %collective-permute-start) | collective-permute-done | bytes 1048608 | tf_op jit(solution)/shard_map/ppermute | solution.py:16
  60.3 1.3 fusion.5
  61.6 1.9 fusion.6
  63.4 1.2 fusion.3
  64.6 46.2 %collective-permute-done.3 = bf16[256,2048]{1,0:T(8,128)(2,1)S(1)} collective-permute-done((bf16[256,2048]{1,0:T(8,128)(2,1)S(1)}, bf16[256,2048]{1,0:T(8,128)(2,1)S(1)}, u32[]{:S(2)}, u32[]{:S(2)}) %collective-permute-start.3) | collective-permute-done | bytes 1048608 | tf_op jit(solution)/shard_map/ppermute | solution.py:16
  110.9 1.2 fusion.2
  112.0 1.9 fusion.1
  113.9 1.8 fusion
  115.7 0.0 all-reduce.4.cloned.1.call-update
  115.8 0.1 select_convert_fusion
  115.9 0.1 mul.138
  115.9 3.0 %collective-permute-done.2 = bf16[256]{0:T(256)(128)(2,1)S(1)} collective-permute-done((bf16[256]{0:T(256)(128)(2,1)S(1)}, bf16[256]{0:T(256)(128)(2,1)S(1)}, u32[]{:S(2)}, u32[]{:S(2)}) %collective-permute-start.2) | collective-permute-done | bytes 544 | tf_op jit(solution)/shard_map/ppermute | solution.py:16
  118.9 1.3 dynamic-slice
  120.2 4.7 %collective-permute-done.5 = bf16[256]{0:T(256)(128)(2,1)S(1)} collective-permute-done((bf16[256]{0:T(256)(128)(2,1)S(1)}, bf16[256]{0:T(256)(128)(2,1)S(1)}, u32[]{:S(2)}, u32[]{:S(2)}) %collective-permute-start.5) | collective-permute-done | bytes 544 | tf_op jit(solution)/shard_map/ppermute | solution.py:16
  124.9 85.0 %all-reduce.4.cloned.1.call-done = (f32[256,256]{1,0:T(8,128)}, f32[256,256]{1,0:T(8,128)}, f32[256,256]{1,0:T(8,128)}, f32[256,256]{1,0:T(8,128)}, f32[256,256]{1,0:T(8,128)}, /*index=5*/f32[256,256]{1,0:T(8,128)}) async-done(((f32[256,256]{1,0:T(8,128)}, f32[256,256]{1,0:T(8,128)}, f32[256,256]{1,0:T(8,128)}, f32[256,256]{1,0:T(8,128)}, f32[256,256]{1,0:T(8,128)}, /*index=5*/f32[256,256]{1,0:T(8,128)}), ...) | async-done | bytes 1572880 | tf_op jit(solution)/shard_map/psum | solution.py:40
  210.0 1.5 multiply_multiply_fusion.2
  211.4 0.3 reshape.74
  211.7 0.3 reshape.75
  212.0 0.2 reduce_sum.28
  212.1 0.2 reduce_sum.29
  212.3 0.3 reshape.73
  212.6 0.2 reduce_sum.27
  212.8 0.1 copy.8
  212.8 52.6 %all-reduce = f32[3,8,8]{1,0,2:T(4,128)S(1)} all-reduce(f32[3,8,8]{1,0,2:T(4,128)S(1)} %copy.8), channel_id=2, replica_groups=mesh['layer'=8,'ex'=16,'width'=4] {'layer'}, use_global_device_ids=true, to_apply=%region_9.0.clone | all-reduce | flops 192 | bytes 1536
  265.4 0.6 constant_dynamic-slice_fusion
  266.0 0.6 copy.9
  (23 shorter events, 0.1 us)
Async XLA Ops:
  6.5 203.4 %all-reduce.4.cloned.1.call-start = ((), (), s32[]{:S(2)}) async-start(), calls=%async_computation | async-start | bytes 3145728 | tf_op jit(solution)/shard_map/psum | solution.py:40
  6.5 42.5 %collective-permute-start.1 = (bf16[256,7168]{1,0:T(8,128)(2,1)}, bf16[256,7168]{1,0:T(8,128)(2,1)S(1)}, u32[]{:S(2)}, u32[]{:S(2)}) collective-permute-start(bf16[256,7168]{1,0:T(8,128)(2,1)} %bitcast.26), channel_id=1, source_target_pairs={{0,4},{4,8},{8,12},{12,16},{16,20},{20,24},{24,28},{28,32},{32,36}... | collective-permute-start | bytes 11010056 | tf_op jit(solution)/shard_map/ppermute | solution.py:16
  6.5 53.8 %collective-permute-start = (bf16[256,2048]{1,0:T(8,128)(2,1)}, bf16[256,2048]{1,0:T(8,128)(2,1)S(1)}, u32[]{:S(2)}, u32[]{:S(2)}) collective-permute-start(bf16[256,2048]{1,0:T(8,128)(2,1)} %bitcast.21), channel_id=1, source_target_pairs={{0,4},{4,8},{8,12},{12,16},{16,20},{20,24},{24,28},{28,32},{32,36}... | collective-permute-start | bytes 3145736 | tf_op jit(solution)/shard_map/ppermute | solution.py:16
  49.1 64.8 %collective-permute-start.4 = (bf16[256,7168]{1,0:T(8,128)(2,1)S(1)}, bf16[256,7168]{1,0:T(8,128)(2,1)S(1)}, u32[]{:S(2)}, u32[]{:S(2)}) collective-permute-start(bf16[256,7168]{1,0:T(8,128)(2,1)S(1)} %collective-permute-done.1), channel_id=1, source_target_pairs={{0,4},{4,8},{8,12},{12,16},{16,20},{20,24},{24,28},{28,32},{32,36}... | collective-permute-start | bytes 11010056 | tf_op jit(solution)/shard_map/ppermute | solution.py:16
  49.1 3.0 %copy-start = (bf16[1,8,32,2048]{3,2,1,0:T(8,128)(2,1)S(1)}, bf16[1,8,32,2048]{3,2,1,0:T(8,128)(2,1)}, u32[]{:S(2)}) copy-start(bf16[1,8,32,2048]{3,2,1,0:T(8,128)(2,1)} %param.6) | copy-start | bytes 3145732
  49.1 3.0 %copy-start.3 = (f32[1,2048]{1,0:T(1,128)S(1)}, f32[1,2048]{1,0:T(1,128)}, u32[]{:S(2)}) copy-start(f32[1,2048]{1,0:T(1,128)} %param.8) | copy-start | bytes 24580
  52.0 9.5 %copy-start.1 = (bf16[1,8,32,7168]{3,2,1,0:T(8,128)(2,1)S(1)}, bf16[1,8,32,7168]{3,2,1,0:T(8,128)(2,1)}, u32[]{:S(2)}) copy-start(bf16[1,8,32,7168]{3,2,1,0:T(8,128)(2,1)} %param.7) | copy-start | bytes 11010052
  60.3 50.6 %collective-permute-start.3 = (bf16[256,2048]{1,0:T(8,128)(2,1)S(1)}, bf16[256,2048]{1,0:T(8,128)(2,1)S(1)}, u32[]{:S(2)}, u32[]{:S(2)}) collective-permute-start(bf16[256,2048]{1,0:T(8,128)(2,1)S(1)} %collective-permute-done), channel_id=1, source_target_pairs={{0,4},{4,8},{8,12},{12,16},{16,20},{20,24},{24,28},{28,32},{32,36}... | collective-permute-start | bytes 3145736 | tf_op jit(solution)/shard_map/ppermute | solution.py:16
  63.4 48.6 %copy-start.2 = (f32[1,7168]{1,0:T(1,128)S(1)}, f32[1,7168]{1,0:T(1,128)}, u32[]{:S(2)}) copy-start(f32[1,7168]{1,0:T(1,128)} %param.9) | copy-start | bytes 86020
  113.9 1.9 copy-start.4
  113.9 1.9 copy-start.5
  115.9 3.0 %collective-permute-start.2 = (bf16[256]{0:T(256)(128)(2,1)S(1)}, bf16[256]{0:T(256)(128)(2,1)S(1)}, u32[]{:S(2)}, u32[]{:S(2)}) collective-permute-start(bf16[256]{0:T(256)(128)(2,1)S(1)} %get-tuple-element.12), channel_id=1, source_target_pairs={{0,4},{4,8},{8,12},{12,16},{16,20},{20,24},{24,28},{28,32},{32,36}... | collective-permute-start | bytes 1544 | tf_op jit(solution)/shard_map/ppermute | solution.py:16
  118.9 6.0 %collective-permute-start.5 = (bf16[256]{0:T(256)(128)(2,1)S(1)}, bf16[256]{0:T(256)(128)(2,1)S(1)}, u32[]{:S(2)}, u32[]{:S(2)}) collective-permute-start(bf16[256]{0:T(256)(128)(2,1)S(1)} %collective-permute-done.2), channel_id=1, source_target_pairs={{0,4},{4,8},{8,12},{12,16},{16,20},{20,24},{24,28},{28,32},{32,36}... | collective-permute-start | bytes 1544 | tf_op jit(solution)/shard_map/ppermute | solution.py:16
Sparse Core Ops, SparseCore 0:
  115.9 94.0 all-reduce.3
where the time goes:
time: 274 us; the launch traced here: 273 us
  waiting for transfers between devices  188 us (69%)
  blocking collectives  52.6 us (19%)
  between operations  13.5 us (5%)
  matrix products  9.2 us (3%)
  other arithmetic  5.23 us (2%)
  local copies, waits for them, and re-layouts  3.47 us (1%)
    ppermute x6, waiting for transfers between devices, from_behind(): return lax.ppermute(value, axis, pairs)  103 us
    psum x1, waiting for transfers between devices, pair_scores(): act_gram, grad_gram = lax.psum((act_gram, grad_gram), 'width')  85 us
    unnamed x1, blocking collectives  52.6 us
    dot_general x3, matrix products, pair_scores(): lax.dot_general(stat_grads, move_grads, contract, preferred_element_type=...  5.56 us
  transfers between devices with their start and end apart: 7, of which 6 were waited for; matrix products, arithmetic and copies ran while one was open for 4% of the time, Pallas kernels for 0%

commit v1 on v0

v1 whole, which is shorter than its diff:
```python
import functools
import math

import jax
import jax.numpy as jnp
from jax import lax
from jax.experimental import pallas as pl
from jax.experimental.pallas import tpu as pltpu
from jax.sharding import PartitionSpec as P

D = 8192
FF = 28672
HOPS = 2
CAP = 176
TALL = 192
OWN = 384
WIDE = 640
TAG = 128
PACK_TILE = 1792
BF16 = jnp.bfloat16
F32 = jnp.float32
VMEM_LIMIT = 48 * 1024 * 1024


def from_behind(value, axis, steps):
    count = lax.axis_size(axis)
    pairs = [(source, (source + steps) % count) for source in range(count)]
    return lax.ppermute(value, axis, pairs)


def plain(activations, gradients, act_scale, grad_scale, weight_rows, tok_slots):
    row_count = weight_rows.shape[0]
    ex_local = row_count // tok_slots
    own_acts = activations[0].reshape(row_count, -1)
    own_grads = gradients[0].reshape(row_count, -1)
    stat_acts = (own_acts.astype(F32) * act_scale[0]).astype(BF16)
    stat_grads = (own_grads.astype(F32) * grad_scale[0]).astype(BF16)
    factor = 1.0 / (math.sqrt(D * FF) * tok_slots)
    contract = (((1,), (1,)), ((), ()))

    def pair_scores(partner):
        move_acts, move_grads, move_weight = partner
        act_gram = lax.dot_general(stat_acts, move_acts, contract, preferred_element_type=F32)
        grad_gram = lax.dot_general(stat_grads, move_grads, contract, preferred_element_type=F32)
        act_gram, grad_gram = lax.psum((act_gram, grad_gram), "width")
        product = act_gram * grad_gram * weight_rows[:, None] * move_weight.astype(F32)[None, :]
        return product.reshape(ex_local, tok_slots, ex_local, tok_slots).sum(axis=(1, 3)) * factor

    partner = (own_acts, own_grads, weight_rows.astype(BF16))
    scores = [pair_scores(partner)]
    for distance in range(HOPS):
        partner = tuple(from_behind(value, "ex", 1) for value in partner)
        scores.append(pair_scores(partner))
    local_ex = lax.broadcasted_iota(jnp.int32, (ex_local, ex_local), 0)
    column_ex = lax.broadcasted_iota(jnp.int32, (ex_local, ex_local), 1)
    scores[0] = scores[0] * (local_ex != column_ex).astype(F32)
    return lax.psum_scatter(jnp.stack(scores), "layer", scatter_dimension=2, tiled=True)


def token_weights(counts_ref, mask_ref):
    ex_local, tok_slots = mask_ref.shape
    rows = ex_local * tok_slots
    position = lax.broadcasted_iota(jnp.int32, (ex_local, tok_slots), 1)
    example = lax.broadcasted_iota(jnp.int32, (ex_local, tok_slots), 0)
    filled = jnp.zeros((ex_local, tok_slots), jnp.int32)
    for place in range(ex_local):
        filled = jnp.where(example == place, counts_ref[place], filled)
    weight = jnp.where((position < filled) & (mask_ref[...] == 1), 1.0, 0.0)
    lane = lax.broadcasted_iota(jnp.int32, (tok_slots, rows), 1)
    slot = lax.broadcasted_iota(jnp.int32, (tok_slots, rows), 0)
    spread = jnp.where(lane % tok_slots == slot, 1.0, 0.0).astype(BF16)
    wide = jnp.dot(weight.astype(BF16), spread, preferred_element_type=F32)
    owner = lax.broadcasted_iota(jnp.int32, (ex_local, rows), 1) // tok_slots
    row = lax.broadcasted_iota(jnp.int32, (ex_local, rows), 0)
    return jnp.sum(jnp.where(owner == row, wide, 0.0), axis=0, keepdims=True)


def pack_acts_kernel(counts_ref, mask_ref, rows_ref, packed_ref, pick_ref, over_ref):
    features, rows = rows_ref.shape[1], rows_ref.shape[0]
    tok_slots = mask_ref.shape[1]
    weights = token_weights(counts_ref, mask_ref)
    before = lax.broadcasted_iota(jnp.int32, (rows, rows), 0)
    upto = lax.broadcasted_iota(jnp.int32, (rows, rows), 1)
    ramp = jnp.where(before <= upto, 1.0, 0.0).astype(BF16)
    lifted = jnp.broadcast_to(weights, (16, rows)).astype(BF16)
    rank = jnp.dot(lifted, ramp, preferred_element_type=F32)[0:1]
    slot = lax.broadcasted_iota(jnp.int32, (CAP, rows), 0).astype(F32) + 1.0
    pick = (jnp.where(slot == rank, 1.0, 0.0) * weights).astype(BF16)
    pick_ref[...] = pick
    total = jnp.broadcast_to(jnp.sum(weights, axis=1, keepdims=True), over_ref.shape)
    over_ref[...] = jnp.where(total > CAP, 1.0, 0.0)
    packed_ref[:, :features] = jnp.dot(pick, rows_ref[...], preferred_element_type=F32).astype(BF16)
    shape = (rows, TAG)
    example = lax.broadcasted_iota(jnp.int32, shape, 0) // tok_slots
    lane = lax.broadcasted_iota(jnp.int32, shape, 1)
    short = jnp.where(lane % 8 == example, 1.0, 0.0)
    long = jnp.where((lane % 32) // 4 == example, 1.0, 0.0)
    tags = jnp.where(lane < 32, short, long).astype(BF16)
    packed_ref[:, features:] = jnp.dot(pick, tags, preferred_element_type=F32).astype(BF16)


def pack_acts(counts, mask, rows):
    count, features = rows.shape
    vmem = pl.BlockSpec(memory_space=pltpu.VMEM)
    return pl.pallas_call(
        pack_acts_kernel,
        in_specs=[pl.BlockSpec(memory_space=pltpu.SMEM), vmem, vmem],
        out_specs=[vmem, vmem, vmem],
        out_shape=[
            jax.ShapeDtypeStruct((CAP, features + TAG), BF16),
            jax.ShapeDtypeStruct((CAP, count), BF16),
            jax.ShapeDtypeStruct((16, TAG), F32),
        ],
        compiler_params=pltpu.CompilerParams(vmem_limit_bytes=VMEM_LIMIT),
        cost_estimate=pl.CostEstimate(
            flops=2 * CAP * count * features, bytes_accessed=4 * count * features, transcendentals=0
        ),
        name="pack_acts",
    )(counts, mask, rows)


def pack_grads_kernel(pick_ref, rows_ref, after_ref, packed_ref):
    del after_ref
    packed_ref[...] = jnp.dot(pick_ref[...], rows_ref[...], preferred_element_type=F32).astype(BF16)


def pack_grads(pick, rows, after, tile=PACK_TILE):
    count, features = rows.shape
    return pl.pallas_call(
        pack_grads_kernel,
        grid=(features // tile,),
        in_specs=[
            pl.BlockSpec((CAP, count), lambda step: (0, 0)),
            pl.BlockSpec((count, tile), lambda step: (0, step)),
            pl.BlockSpec(memory_space=pl.ANY),
        ],
        out_specs=pl.BlockSpec((CAP, tile), lambda step: (0, step)),
        out_shape=jax.ShapeDtypeStruct((CAP, features), BF16),
        compiler_params=pltpu.CompilerParams(vmem_limit_bytes=VMEM_LIMIT),
        cost_estimate=pl.CostEstimate(
            flops=40 * CAP * count * features, bytes_accessed=4 * count * features, transcendentals=0
        ),
        name="pack_grads",
    )(pick, rows, after)


def add_grams(parity, own_ref, near_ref, far_ref, scale_ref, gram_ref):
    contract = (((1,), (1,)), ((), ()))

    def scaled(ref):
        return (ref[...].astype(F32) * scale_ref[...]).astype(BF16)

    def pairs(left_ref, last_ref):
        right = jnp.concatenate([near_ref[...], last_ref[...]], axis=0)
        gram_ref[:CAP, : 2 * CAP] += lax.dot_general(
            scaled(left_ref), right, contract, preferred_element_type=F32
        )

    gram_ref[:CAP, OWN : OWN + CAP] += lax.dot_general(
        scaled(own_ref), own_ref[...], contract, preferred_element_type=F32
    )

    @pl.when(parity == 1)
    def _():
        pairs(own_ref, far_ref)

    @pl.when(parity == 0)
    def _():
        pairs(far_ref, own_ref)


def gram_kernel(own_ref, near_ref, far_ref, scale_ref, parity_ref, note_ref, gram_ref, said_ref):
    @pl.when(pl.program_id(0) == 0)
    def _():
        gram_ref[...] = jnp.zeros_like(gram_ref)
        said_ref[...] = jnp.max(note_ref[...], axis=0, keepdims=True)

    add_grams(parity_ref[0], own_ref, near_ref, far_ref, scale_ref, gram_ref)


def gram(own, near, far, scale, parity, note, tile, weight):
    features = scale.shape[1]
    block = pl.BlockSpec((CAP, tile), lambda step: (0, step))
    return pl.pallas_call(
        gram_kernel,
        grid=(features // tile,),
        in_specs=[
            block,
            block,
            block,
            pl.BlockSpec((1, tile), lambda step: (0, step)),
            pl.BlockSpec(memory_space=pltpu.SMEM),
            pl.BlockSpec(note.shape, lambda step: (0, 0)),
        ],
        out_specs=[
            pl.BlockSpec((TALL, WIDE), lambda step: (0, 0)),
            pl.BlockSpec((1, TAG), lambda step: (0, 0)),
        ],
        out_shape=[jax.ShapeDtypeStruct((TALL, WIDE), F32), jax.ShapeDtypeStruct((1, TAG), F32)],
        compiler_params=pltpu.CompilerParams(vmem_limit_bytes=VMEM_LIMIT),
        cost_estimate=pl.CostEstimate(
            flops=weight * 6 * 256 * 256 * features, bytes_accessed=6 * CAP * features, transcendentals=0
        ),
        name="gram",
    )(own, near, far, scale, parity, note)


def spread_kernel(parts_ref, out_ref):
    total = parts_ref[0]
    for part in range(1, parts_ref.shape[0]):
        total = total + parts_ref[part]
    for part in range(out_ref.shape[0]):
        out_ref[part] = total


def sum_and_spread(parts):
    return pl.pallas_call(
        spread_kernel,
        out_shape=jax.ShapeDtypeStruct(parts.shape, F32),
        compiler_params=pltpu.CompilerParams(vmem_limit_bytes=VMEM_LIMIT),
        name="sum_and_spread",
    )(parts)


def exact_dot(left, one_hot, contract):
    total = None
    for _ in range(3):
        part = left.astype(BF16)
        left = left - part.astype(F32)
        term = lax.dot_general(part, one_hot, contract, preferred_element_type=F32)
        total = term if total is None else total + term
    return total


def finish_kernel(
    factor, grad_ref, act_ref, parity_ref, own_tag_ref, near_tag_ref, far_tag_ref, out_ref, tag_ref
):
    product = grad_ref[...] * act_ref[...]
    lane = lax.broadcasted_iota(jnp.int32, (CAP, TAG), 1) // 32
    odd = (parity_ref[0] == 1).astype(F32)
    own, near, far = (ref[...].astype(F32) for ref in (own_tag_ref, near_tag_ref, far_tag_ref))
    last = odd * far + (1.0 - odd) * own
    left = odd * own + (1.0 - odd) * far
    tag_ref[...] = jnp.zeros_like(tag_ref)
    tag_ref[:CAP] = jnp.where(lane == 1, near, 0.0).astype(BF16)
    tag_ref[CAP : 2 * CAP] = jnp.where(lane == 2, last, 0.0).astype(BF16)
    tag_ref[OWN : OWN + CAP] = jnp.where(lane == 3, own, 0.0).astype(BF16)
    by_column = exact_dot(product, tag_ref[...], (((1,), (0,)), ((), ())))[:CAP]
    by_row = (((0,), (0,)), ((), ()))
    pairs = exact_dot(by_column, left.astype(BF16), by_row)
    selves = exact_dot(by_column, own.astype(BF16), by_row)
    shape = (32, TAG)
    column = lax.broadcasted_iota(jnp.int32, shape, 0) // 4
    place = lax.broadcasted_iota(jnp.int32, shape, 1)
    out_ref[...] = factor * (
        jnp.where((place < 8) & (place != column), selves[96:128], 0.0)
        + jnp.where((place >= 8) & (place < 16), pairs[32:64], 0.0)
        + jnp.where((place >= 16) & (place < 24), pairs[64:96], 0.0)
    )


def finish(factor, grad_gram, act_gram, parity, tags):
    tag_at = tags[0].shape[1] // TAG - 1
    whole = pl.BlockSpec((TALL, WIDE), lambda step: (0, 0))
    tag = pl.BlockSpec((CAP, TAG), lambda step: (0, tag_at))
    return pl.pallas_call(
        functools.partial(finish_kernel, factor),
        grid=(1,),
        in_specs=[whole, whole, pl.BlockSpec(memory_space=pltpu.SMEM), tag, tag, tag],
        out_specs=pl.BlockSpec((32, TAG), lambda step: (0, 0)),
        out_shape=jax.ShapeDtypeStruct((32, TAG), F32),
        scratch_shapes=[pltpu.VMEM((WIDE, TAG), BF16)],
        compiler_params=pltpu.CompilerParams(vmem_limit_bytes=VMEM_LIMIT),
        name="finish",
    )(grad_gram, act_gram, parity, *tags)


def far_swap(value):
    count = lax.axis_size("ex")
    pairs = [(e, (e + (2 if e % 2 else -2)) % count) for e in range(count)]
    return lax.ppermute(value, "ex", pairs)


def near_swap(value):
    count = lax.axis_size("ex")
    return lax.ppermute(value, "ex", [(e, e ^ 1) for e in range(count)])


def sum_over_width(value):
    parts = lax.axis_size("width")
    split = value.reshape(parts, TALL // parts, WIDE)
    spread = sum_and_spread(lax.all_to_all(split, "width", 0, 0))
    return lax.all_to_all(spread, "width", 0, 0).reshape(TALL, WIDE)


def local(activations, gradients, act_scale, grad_scale, counts, loss_mask):
    ex_local, tok_slots = loss_mask.shape
    row_count = ex_local * tok_slots
    own_acts = activations[0].reshape(row_count, -1)
    own_grads = gradients[0].reshape(row_count, -1)
    positions = lax.broadcasted_iota(jnp.int32, (ex_local, tok_slots), 1)
    token_weight = (positions < counts[:, None]).astype(jnp.int32) * loss_mask
    weight_rows = token_weight.astype(F32).reshape(row_count)
    parity = (lax.axis_index("ex") % 2).astype(jnp.int32).reshape(1)
    factor = 1.0 / (math.sqrt(D * FF) * tok_slots)

    acts, pick, over = pack_acts(counts, loss_mask, own_acts)
    far_acts, near_acts = far_swap(acts), near_swap(acts)
    grads = pack_grads(pick, own_grads, near_acts)
    far_grads, near_grads = far_swap(grads), near_swap(grads)
    over_all = lax.all_to_all(over, "ex", 0, 0, tiled=True)

    act_gram, _ = gram(acts, near_acts, far_acts, act_scale, parity, over, 1024, 300)
    act_gram = sum_over_width(act_gram)
    grad_gram, most = gram(grads, near_grads, far_grads, grad_scale, parity, over_all, PACK_TILE, 1)
    crowded = most[0, 0] > 0.0
    scores = finish(factor, grad_gram, act_gram, parity, (acts, near_acts, far_acts))
    mine = lax.all_to_all(scores, ("layer", "width"), 0, 0, tiled=True).sum(axis=0)
    ahead = from_behind(mine, "ex", 2)
    place = lax.broadcasted_iota(jnp.int32, mine.shape, 0)
    kept = jnp.where((place < 8) | (parity[0] == 1), mine, ahead)
    quick = kept[: 8 * (HOPS + 1)].reshape(HOPS + 1, ex_local, 1)
    return lax.cond(
        crowded,
        lambda: plain(activations, gradients, act_scale, grad_scale, weight_rows, tok_slots),
        lambda: quick,
    )


def solution(mesh):
    in_specs = (
        P("layer", "ex", None, "width"),
        P("layer", "ex", None, "width"),
        P("layer", "width"),
        P("layer", "width"),
        P("ex"),
        P("ex", None),
    )
    out_specs = P(None, "ex", "layer")
    return jax.shard_map(local, mesh=mesh, in_specs=in_specs, out_specs=out_specs, check_vma=False)
```

time: 274 us -> 117 us (0.43)
  the two profiles are of different devices: /device:TPU:8 before, /device:TPU:2 now
where the time goes in v1:
time: 117 us; the launch traced here: 116 us
  blocking collectives  39.4 us (34%)
  starting transfers between devices  25 us (21%)
  waiting for transfers between devices  18.8 us (16%)
  Pallas kernels  17.3 us (15%)
  between operations  13.6 us (12%)
  local copies, waits for them, and re-layouts  2.01 us (2%)
    all_to_all x1, blocking collectives, sum_over_width(): spread = sum_and_spread(lax.all_to_all(split, 'width', 0, 0))  20.3 us
    all_to_all x1, blocking collectives, local(): lax.all_to_all(scores, ('layer', 'width'), 0, 0, tiled=True).sum(axis=0)  19.1 us
    pallas_call x2, Pallas kernels, gram(): pl.pallas_call(gram_kernel, grid=(features // tile,), in_specs=[block, bl...  8.87 us
    ppermute x2, starting transfers between devices, far_swap(): return lax.ppermute(value, 'ex', pairs)  8.64 us
    all_to_all x1, waiting for transfers between devices, sum_over_width(): return lax.all_to_all(spread, 'width', 0, 0).reshape(TALL, WIDE)  7.99 us
    all_to_all x1, waiting for transfers between devices, local(): over_all = lax.all_to_all(over, 'ex', 0, 0, tiled=True)  6.73 us
    all_to_all x1, starting transfers between devices, local(): over_all = lax.all_to_all(over, 'ex', 0, 0, tiled=True)  6.68 us
    pallas_call x1, Pallas kernels, pack_grads(): pl.pallas_call(pack_grads_kernel, grid=(features // tile,), in_specs=[pl....  4.79 us
  transfers between devices with their start and end apart: 7, of which 3 were waited for; matrix products, arithmetic and copies ran while one was open for 0% of the time, Pallas kernels for 12%

profile of v1, /device:TPU:2, one launch (start us, length us, event | category | flops | bytes accessed | tf_op | source)
XLA Modules:
  0.0 116.4 jit_solution(8808131498401555836)
XLA Ops:
  6.5 0.7 copy-done
  7.2 0.7 copy-done.2
  7.9 2.0 %pack_acts.1 = (bf16[176,2176]{1,0:T(8,128)(2,1)S(1)}, bf16[176,256]{1,0:T(8,128)(2,1)S(1)}, f32[16,128]{1,0:T(8,128)}) custom-call(s32[8]{0:T(128)S(1)} %copy-done.2, s32[8,32]{1,0:T(8,128)S(1)} %copy-done, bf16[256,2048]{1,0:T(8,128)(2,1)} %bitcast.41), custom_call_target="tpu_custom_call" | custom-call | flops 184549376 | bytes 2097152 | tf_op jit(solution)/shard_map/pack_acts/pallas_call | solution.py:105
  9.9 1.9 %collective-permute-start.6 = (bf16[176,2176]{1,0:T(8,128)(2,1)S(1)}, bf16[176,2176]{1,0:T(8,128)(2,1)S(1)}, u32[]{:S(2)}, u32[]{:S(2)}) collective-permute-start(bf16[176,2176]{1,0:T(8,128)(2,1)S(1)} %get-tuple-element.56.own_ref.own_tag_ref), channel_id=1, source_target_pairs={{0,4},{4,0},{8,12},{12,8},{16,20},{20,16},{24,28},{28,24},{32,36},... | collective-permute-start | bytes 2297864 | tf_op jit(solution)/shard_map/ppermute | solution.py:286
  11.8 5.4 %collective-permute-start.9 = (bf16[176,2176]{1,0:T(8,128)(2,1)S(1)}, bf16[176,2176]{1,0:T(8,128)(2,1)S(1)}, u32[]{:S(2)}, u32[]{:S(2)}) collective-permute-start(bf16[176,2176]{1,0:T(8,128)(2,1)S(1)} %get-tuple-element.56.own_ref.own_tag_ref), channel_id=1, source_target_pairs={{0,56},{4,12},{8,0},{12,20},{16,8},{20,28},{24,16},{28,36},{32,24}... | collective-permute-start | bytes 2297864 | tf_op jit(solution)/shard_map/ppermute | solution.py:281
  17.2 0.0 collective-permute-done.6.after_ref.near_ref.near_tag_ref
  17.2 0.0 copy-start.7
  17.2 4.8 %pack_grads.1.own_ref = bf16[176,7168]{1,0:T(8,128)(2,1)} custom-call(bf16[176,256]{1,0:T(8,128)(2,1)S(1)} %get-tuple-element.55.pick_ref, bf16[256,7168]{1,0:T(8,128)(2,1)} %bitcast.47, bf16[176,2176]{1,0:T(8,128)(2,1)S(1)} %collective-permute-done.6.after_ref.near_ref.near_tag_ref), custom_call_target="tpu_custom_call" | custom-call | flops 12918456320 | bytes 7340032 | tf_op jit(solution)/shard_map/pack_grads/pallas_call | solution.py:129
  22.0 1.9 %collective-permute-start.7 = (bf16[176,7168]{1,0:T(8,128)(2,1)}, bf16[176,7168]{1,0:T(8,128)(2,1)}, u32[]{:S(2)}, u32[]{:S(2)}) collective-permute-start(bf16[176,7168]{1,0:T(8,128)(2,1)} %pack_grads.1.own_ref), channel_id=1, source_target_pairs={{0,4},{4,0},{8,12},{12,8},{16,20},{20,16},{24,28},{28,24},{32,36},... | collective-permute-start | bytes 7569416 | tf_op jit(solution)/shard_map/ppermute | solution.py:286
  24.0 3.3 %collective-permute-start.8 = (bf16[176,7168]{1,0:T(8,128)(2,1)}, bf16[176,7168]{1,0:T(8,128)(2,1)}, u32[]{:S(2)}, u32[]{:S(2)}) collective-permute-start(bf16[176,7168]{1,0:T(8,128)(2,1)} %pack_grads.1.own_ref), channel_id=1, source_target_pairs={{0,56},{4,12},{8,0},{12,20},{16,8},{20,28},{24,16},{28,36},{32,24}... | collective-permute-start | bytes 7569416 | tf_op jit(solution)/shard_map/ppermute | solution.py:281
  27.2 0.0 collective-permute-done.9.far_ref.far_tag_ref
  27.2 0.0 copy-start.6
  27.3 2.8 %gram.3 = (f32[192,640]{1,0:T(8,128)S(1)}, f32[1,128]{1,0:T(1,128)}) custom-call(bf16[176,2176]{1,0:T(8,128)(2,1)S(1)} %get-tuple-element.56.own_ref.own_tag_ref, bf16[176,2176]{1,0:T(8,128)(2,1)S(1)} %collective-permute-done.6.after_ref.near_ref.near_tag_ref, bf16[176,2176]{1,0:T(8,128)(2,1)S(1)} %collective-permute-done.9.far_ref.far_tag_ref, ...), custom_call_target="tpu_custom_call" | custom-call | flops 241591910400 | bytes 2162688 | tf_op jit(solution)/shard_map/gram/pallas_call | solution.py:184
  30.1 20.3 %all_to_all.30.parts_ref = f32[4,48,640]{2,1,0:T(8,128)S(1)} all-to-all(f32[4,48,640]{2,1,0:T(8,128)S(1)} %bitcast.37), channel_id=1, replica_groups=mesh['layer'=8,'ex'=16,'width'=4] {'width'}, dimensions={0} | all-to-all | bytes 983040 | tf_op jit(solution)/shard_map/all_to_all | solution.py:292
  50.4 6.7 %all-to-all-start = ((f32[16,1,128]{2,1,0:T(1,128)}), f32[16,1,128]{2,1,0:T(1,128)S(1)}, u32[]{:S(2)}, u32[]{:S(2)}) async-start(f32[16,1,128]{2,1,0:T(1,128)} %bitcast.13), calls=%async_computation | async-start | bytes 16384 | tf_op jit(solution)/shard_map/all_to_all | solution.py:311
  57.1 0.8 sum_and_spread.1
  57.9 6.7 %all-to-all-done = f32[16,1,128]{2,1,0:T(1,128)S(1)} async-done(((f32[16,1,128]{2,1,0:T(1,128)}), f32[16,1,128]{2,1,0:T(1,128)S(1)}, u32[]{:S(2)}, u32[]{:S(2)}) %all-to-all-start) | async-done | bytes 8224 | tf_op jit(solution)/shard_map/all_to_all | solution.py:311
  64.7 3.5 %all-to-all-start.2 = ((f32[4,48,640]{2,1,0:T(8,128)}), f32[4,48,640]{2,1,0:T(8,128)S(1)}, u32[]{:S(2)}, u32[]{:S(2)}) async-start(f32[4,48,640]{2,1,0:T(8,128)} %sum_and_spread.1), calls=%async_computation.2 | async-start | bytes 983040 | tf_op jit(solution)/shard_map/all_to_all | solution.py:293
  68.2 0.0 copy-start.1
  68.2 0.0 copy-start.3
  68.2 6.0 %gram.2 = (f32[192,640]{1,0:T(8,128)S(1)}, f32[1,128]{1,0:T(1,128)S(1)}) custom-call(bf16[176,7168]{1,0:T(8,128)(2,1)} %pack_grads.1.own_ref, bf16[176,7168]{1,0:T(8,128)(2,1)} %collective-permute-done.7.near_ref, bf16[176,7168]{1,0:T(8,128)(2,1)} %collective-permute-done.8.far_ref, f32[1,7168]{1,0:T(1,128)S(1)} %copy-done.6, s32[1]{0:T(128)} %bitcast.11.parity_ref, ...), custom_call_target="tpu_custom_call" | custom-call | flops 2818572288 | bytes 7569408 | tf_op jit(solution)/shard_map/gram/pallas_call | solution.py:184
  74.2 8.0 %all-to-all-done.2 = f32[4,48,640]{2,1,0:T(8,128)S(1)} async-done(((f32[4,48,640]{2,1,0:T(8,128)}), f32[4,48,640]{2,1,0:T(8,128)S(1)}, u32[]{:S(2)}, u32[]{:S(2)}) %all-to-all-start.2) | async-done | bytes 491552 | tf_op jit(solution)/shard_map/all_to_all | solution.py:293
  82.2 0.7 finish.1
  83.0 19.1 %all_to_all.31 = f32[32,1,128]{2,1,0:T(1,128)S(1)} all-to-all(f32[32,1,128]{2,1,0:T(1,128)S(1)} %bitcast.38), channel_id=1, replica_groups=mesh['layer'=8,'ex'=16,'width'=4] {'layer','width'}, dimensions={0} | all-to-all | bytes 32768 | tf_op jit(solution)/shard_map/all_to_all | solution.py:318
  102.1 0.1 reduce_sum.36
  102.1 2.4 %collective-permute-start.10 = (f32[128]{0:T(128)S(1)}, f32[128]{0:T(128)S(1)}, u32[]{:S(2)}, u32[]{:S(2)}) collective-permute-start(f32[128]{0:T(128)S(1)} %reduce_sum.36), channel_id=1, source_target_pairs={{0,8},{4,12},{8,16},{12,20},{16,24},{20,28},{24,32},{28,36},{32,40... | collective-permute-start | bytes 1544 | tf_op jit(solution)/shard_map/ppermute | solution.py:28
  104.6 0.1 select_convert_fusion
  104.7 4.1 %collective-permute-done.10 = f32[128]{0:T(128)S(1)} collective-permute-done((f32[128]{0:T(128)S(1)}, f32[128]{0:T(128)S(1)}, u32[]{:S(2)}, u32[]{:S(2)}) %collective-permute-start.10) | collective-permute-done | bytes 544 | tf_op jit(solution)/shard_map/ppermute | solution.py:28
  108.8 0.2 conditional.1
  108.8 0.1 slice.18
  109.0 0.0 copy-start.8
  109.1 0.6 copy-done.8
  (10 shorter events, 0.0 us)
Async XLA Ops:
  6.5 0.7 copy-start
  7.2 0.7 copy-start.2
  9.9 7.3 %collective-permute-start.6 = (bf16[176,2176]{1,0:T(8,128)(2,1)S(1)}, bf16[176,2176]{1,0:T(8,128)(2,1)S(1)}, u32[]{:S(2)}, u32[]{:S(2)}) collective-permute-start(bf16[176,2176]{1,0:T(8,128)(2,1)S(1)} %get-tuple-element.56.own_ref.own_tag_ref), channel_id=1, source_target_pairs={{0,4},{4,0},{8,12},{12,8},{16,20},{20,16},{24,28},{28,24},{32,36},... | collective-permute-start | bytes 2297864 | tf_op jit(solution)/shard_map/ppermute | solution.py:286
  11.8 15.4 %collective-permute-start.9 = (bf16[176,2176]{1,0:T(8,128)(2,1)S(1)}, bf16[176,2176]{1,0:T(8,128)(2,1)S(1)}, u32[]{:S(2)}, u32[]{:S(2)}) collective-permute-start(bf16[176,2176]{1,0:T(8,128)(2,1)S(1)} %get-tuple-element.56.own_ref.own_tag_ref), channel_id=1, source_target_pairs={{0,56},{4,12},{8,0},{12,20},{16,8},{20,28},{24,16},{28,36},{32,24}... | collective-permute-start | bytes 2297864 | tf_op jit(solution)/shard_map/ppermute | solution.py:281
  17.2 10.0 %copy-start.7 = (f32[1,2048]{1,0:T(1,128)S(1)}, f32[1,2048]{1,0:T(1,128)}, u32[]{:S(2)}) copy-start(f32[1,2048]{1,0:T(1,128)} %scale_ref.3) | copy-start | bytes 24580
  22.0 46.1 %collective-permute-start.7 = (bf16[176,7168]{1,0:T(8,128)(2,1)}, bf16[176,7168]{1,0:T(8,128)(2,1)}, u32[]{:S(2)}, u32[]{:S(2)}) collective-permute-start(bf16[176,7168]{1,0:T(8,128)(2,1)} %pack_grads.1.own_ref), channel_id=1, source_target_pairs={{0,4},{4,0},{8,12},{12,8},{16,20},{20,16},{24,28},{28,24},{32,36},... | collective-permute-start | bytes 7569416 | tf_op jit(solution)/shard_map/ppermute | solution.py:286
  24.0 44.2 %collective-permute-start.8 = (bf16[176,7168]{1,0:T(8,128)(2,1)}, bf16[176,7168]{1,0:T(8,128)(2,1)}, u32[]{:S(2)}, u32[]{:S(2)}) collective-permute-start(bf16[176,7168]{1,0:T(8,128)(2,1)} %pack_grads.1.own_ref), channel_id=1, source_target_pairs={{0,56},{4,12},{8,0},{12,20},{16,8},{20,28},{24,16},{28,36},{32,24}... | collective-permute-start | bytes 7569416 | tf_op jit(solution)/shard_map/ppermute | solution.py:281
  27.2 40.9 %copy-start.6 = (f32[1,7168]{1,0:T(1,128)S(1)}, f32[1,7168]{1,0:T(1,128)}, u32[]{:S(2)}) copy-start(f32[1,7168]{1,0:T(1,128)} %scale_ref.2) | copy-start | bytes 86020
  50.4 14.3 %all-to-all-start = ((f32[16,1,128]{2,1,0:T(1,128)}), f32[16,1,128]{2,1,0:T(1,128)S(1)}, u32[]{:S(2)}, u32[]{:S(2)}) async-start(f32[16,1,128]{2,1,0:T(1,128)} %bitcast.13), calls=%async_computation | async-start | bytes 16384 | tf_op jit(solution)/shard_map/all_to_all | solution.py:311
  64.7 17.5 %all-to-all-start.2 = ((f32[4,48,640]{2,1,0:T(8,128)}), f32[4,48,640]{2,1,0:T(8,128)S(1)}, u32[]{:S(2)}, u32[]{:S(2)}) async-start(f32[4,48,640]{2,1,0:T(8,128)} %sum_and_spread.1), calls=%async_computation.2 | async-start | bytes 983040 | tf_op jit(solution)/shard_map/all_to_all | solution.py:293
  68.2 36.4 %copy-start.1 = (s32[8,32]{1,0:T(8,128)S(1)}, s32[8,32]{1,0:T(8,128)}, u32[]{:S(2)}) copy-start(s32[8,32]{1,0:T(8,128)} %mask_ref.1) | copy-start | bytes 3076
  68.2 36.4 %copy-start.3 = (s32[8]{0:T(128)S(1)}, s32[8]{0:T(128)}, u32[]{:S(2)}) copy-start(s32[8]{0:T(128)} %counts_ref.1) | copy-start | bytes 100
  102.1 6.6 %collective-permute-start.10 = (f32[128]{0:T(128)S(1)}, f32[128]{0:T(128)S(1)}, u32[]{:S(2)}, u32[]{:S(2)}) collective-permute-start(f32[128]{0:T(128)S(1)} %reduce_sum.36), channel_id=1, source_target_pairs={{0,8},{4,12},{8,16},{12,20},{16,24},{20,28},{24,32},{28,36},{32,40... | collective-permute-start | bytes 1544 | tf_op jit(solution)/shard_map/ppermute | solution.py:28
  109.0 0.6 copy-start.8

commit v2 on v1

--- a/solution.py
+++ b/solution.py
@@ -16,16 +16,24 @@
 OWN = 384
 WIDE = 640
 TAG = 128
-PACK_TILE = 1792
+TILE = 3584
 BF16 = jnp.bfloat16
 F32 = jnp.float32
-VMEM_LIMIT = 48 * 1024 * 1024
+VMEM_LIMIT = 24 * 1024 * 1024
 
 
 def from_behind(value, axis, steps):
     count = lax.axis_size(axis)
     pairs = [(source, (source + steps) % count) for source in range(count)]
     return lax.ppermute(value, axis, pairs)
+
+
+def butterfly_sum(value, axis):
+    count, step = lax.axis_size(axis), 1
+    while step < count:
+        value = value + lax.ppermute(value, axis, [(place, place ^ step) for place in range(count)])
+        step *= 2
+    return value
 
 
 def plain(activations, gradients, act_scale, grad_scale, weight_rows, tok_slots):
@@ -42,7 +50,7 @@
         move_acts, move_grads, move_weight = partner
         act_gram = lax.dot_general(stat_acts, move_acts, contract, preferred_element_type=F32)
         grad_gram = lax.dot_general(stat_grads, move_grads, contract, preferred_element_type=F32)
-        act_gram, grad_gram = lax.psum((act_gram, grad_gram), "width")
+        act_gram, grad_gram = butterfly_sum(act_gram, "width"), butterfly_sum(grad_gram, "width")
         product = act_gram * grad_gram * weight_rows[:, None] * move_weight.astype(F32)[None, :]
         return product.reshape(ex_local, tok_slots, ex_local, tok_slots).sum(axis=(1, 3)) * factor
 
@@ -54,7 +62,9 @@
     local_ex = lax.broadcasted_iota(jnp.int32, (ex_local, ex_local), 0)
     column_ex = lax.broadcasted_iota(jnp.int32, (ex_local, ex_local), 1)
     scores[0] = scores[0] * (local_ex != column_ex).astype(F32)
-    return lax.psum_scatter(jnp.stack(scores), "layer", scatter_dimension=2, tiled=True)
+    summed = butterfly_sum(jnp.stack(scores), "layer")
+    column = lax.axis_index("layer") * (ex_local // lax.axis_size("layer"))
+    return lax.dynamic_slice_in_dim(summed, column, ex_local // lax.axis_size("layer"), axis=2)
 
 
 def token_weights(counts_ref, mask_ref):
@@ -104,7 +114,12 @@
     vmem = pl.BlockSpec(memory_space=pltpu.VMEM)
     return pl.pallas_call(
         pack_acts_kernel,
-        in_specs=[pl.BlockSpec(memory_space=pltpu.SMEM), vmem, vmem],
+        grid=(1,),
+        in_specs=[
+            pl.BlockSpec(memory_space=pltpu.SMEM),
+            pl.BlockSpec(mask.shape, lambda step: (0, 0)),
+            pl.BlockSpec(rows.shape, lambda step: (0, 0)),
+        ],
         out_specs=[vmem, vmem, vmem],
         out_shape=[
             jax.ShapeDtypeStruct((CAP, features + TAG), BF16),
@@ -124,17 +139,17 @@
     packed_ref[...] = jnp.dot(pick_ref[...], rows_ref[...], preferred_element_type=F32).astype(BF16)
 
 
-def pack_grads(pick, rows, after, tile=PACK_TILE):
+def pack_grads(pick, rows, after):
     count, features = rows.shape
     return pl.pallas_call(
         pack_grads_kernel,
-        grid=(features // tile,),
+        grid=(features // TILE,),
         in_specs=[
             pl.BlockSpec((CAP, count), lambda step: (0, 0)),
-            pl.BlockSpec((count, tile), lambda step: (0, step)),
+            pl.BlockSpec((count, TILE), lambda step: (0, step)),
             pl.BlockSpec(memory_space=pl.ANY),
         ],
-        out_specs=pl.BlockSpec((CAP, tile), lambda step: (0, step)),
+        out_specs=pl.BlockSpec((CAP, TILE), lambda step: (0, step)),
         out_shape=jax.ShapeDtypeStruct((CAP, features), BF16),
         compiler_params=pltpu.CompilerParams(vmem_limit_bytes=VMEM_LIMIT),
         cost_estimate=pl.CostEstimate(
@@ -144,42 +159,36 @@
     )(pick, rows, after)
 
 
-def add_grams(parity, own_ref, near_ref, far_ref, scale_ref, gram_ref):
+def gram_kernel(far_ref, near_ref, own_ref, scale_ref, parity_ref, gram_ref):
     contract = (((1,), (1,)), ((), ()))
 
-    def scaled(ref):
-        return (ref[...].astype(F32) * scale_ref[...]).astype(BF16)
-
-    def pairs(left_ref, last_ref):
-        right = jnp.concatenate([near_ref[...], last_ref[...]], axis=0)
-        gram_ref[:CAP, : 2 * CAP] += lax.dot_general(
-            scaled(left_ref), right, contract, preferred_element_type=F32
-        )
-
-    gram_ref[:CAP, OWN : OWN + CAP] += lax.dot_general(
-        scaled(own_ref), own_ref[...], contract, preferred_element_type=F32
-    )
-
-    @pl.when(parity == 1)
-    def _():
-        pairs(own_ref, far_ref)
-
-    @pl.when(parity == 0)
-    def _():
-        pairs(far_ref, own_ref)
-
-
-def gram_kernel(own_ref, near_ref, far_ref, scale_ref, parity_ref, note_ref, gram_ref, said_ref):
     @pl.when(pl.program_id(0) == 0)
     def _():
         gram_ref[...] = jnp.zeros_like(gram_ref)
-        said_ref[...] = jnp.max(note_ref[...], axis=0, keepdims=True)
-
-    add_grams(parity_ref[0], own_ref, near_ref, far_ref, scale_ref, gram_ref)
-
-
-def gram(own, near, far, scale, parity, note, tile, weight):
+
+    def scaled(ref):
+        return (ref[...].astype(F32) * scale_ref[...]).astype(BF16)
+
+    def add(columns, left, right):
+        gram_ref[:CAP, columns] += lax.dot_general(left, right, contract, preferred_element_type=F32)
+
+    pair, alone = slice(0, 2 * CAP), slice(OWN, OWN + CAP)
+
+    @pl.when(parity_ref[0] == 1)
+    def _():
+        left = scaled(own_ref)
+        add(pair, left, jnp.concatenate([near_ref[...], far_ref[...]], axis=0))
+        add(alone, left, own_ref[...])
+
+    @pl.when(parity_ref[0] == 0)
+    def _():
+        add(pair, scaled(far_ref), jnp.concatenate([near_ref[...], own_ref[...]], axis=0))
+        add(alone, scaled(own_ref), own_ref[...])
+
+
+def gram(own, near, far, scale, parity, weight):
     features = scale.shape[1]
+    tile = min(features, TILE)
     block = pl.BlockSpec((CAP, tile), lambda step: (0, step))
     return pl.pallas_call(
         gram_kernel,
@@ -190,36 +199,37 @@
             block,
             pl.BlockSpec((1, tile), lambda step: (0, step)),
             pl.BlockSpec(memory_space=pltpu.SMEM),
-            pl.BlockSpec(note.shape, lambda step: (0, 0)),
-        ],
-        out_specs=[
-            pl.BlockSpec((TALL, WIDE), lambda step: (0, 0)),
-            pl.BlockSpec((1, TAG), lambda step: (0, 0)),
-        ],
-        out_shape=[jax.ShapeDtypeStruct((TALL, WIDE), F32), jax.ShapeDtypeStruct((1, TAG), F32)],
+        ],
+        out_specs=pl.BlockSpec((TALL, WIDE), lambda step: (0, 0)),
+        out_shape=jax.ShapeDtypeStruct((TALL, WIDE), F32),
         compiler_params=pltpu.CompilerParams(vmem_limit_bytes=VMEM_LIMIT),
         cost_estimate=pl.CostEstimate(
             flops=weight * 6 * 256 * 256 * features, bytes_accessed=6 * CAP * features, transcendentals=0
         ),
         name="gram",
-    )(own, near, far, scale, parity, note)
-
-
-def spread_kernel(parts_ref, out_ref):
+    )(far, near, own, scale, parity)
+
+
+def spread_kernel(parts_ref, note_ref, out_ref, said_ref):
     total = parts_ref[0]
     for part in range(1, parts_ref.shape[0]):
         total = total + parts_ref[part]
+    rounded = total.astype(BF16)
     for part in range(out_ref.shape[0]):
-        out_ref[part] = total
-
-
-def sum_and_spread(parts):
+        out_ref[part] = rounded
+    said_ref[...] = jnp.max(note_ref[...], axis=0, keepdims=True)
+
+
+def sum_and_spread(parts, note):
     return pl.pallas_call(
         spread_kernel,
-        out_shape=jax.ShapeDtypeStruct(parts.shape, F32),
+        out_shape=[
+            jax.ShapeDtypeStruct(parts.shape, BF16),
+            jax.ShapeDtypeStruct((1, note.shape[1]), F32),
+        ],
         compiler_params=pltpu.CompilerParams(vmem_limit_bytes=VMEM_LIMIT),
         name="sum_and_spread",
-    )(parts)
+    )(parts, note)
 
 
 def exact_dot(left, one_hot, contract):
@@ -235,7 +245,7 @@
 def finish_kernel(
     factor, grad_ref, act_ref, parity_ref, own_tag_ref, near_tag_ref, far_tag_ref, out_ref, tag_ref
 ):
-    product = grad_ref[...] * act_ref[...]
+    product = grad_ref[...] * act_ref[...].astype(F32)
     lane = lax.broadcasted_iota(jnp.int32, (CAP, TAG), 1) // 32
     odd = (parity_ref[0] == 1).astype(F32)
     own, near, far = (ref[...].astype(F32) for ref in (own_tag_ref, near_tag_ref, far_tag_ref))
@@ -286,11 +296,11 @@
     return lax.ppermute(value, "ex", [(e, e ^ 1) for e in range(count)])
 
 
-def sum_over_width(value):
+def sum_over_width(value, note):
     parts = lax.axis_size("width")
     split = value.reshape(parts, TALL // parts, WIDE)
-    spread = sum_and_spread(lax.all_to_all(split, "width", 0, 0))
-    return lax.all_to_all(spread, "width", 0, 0).reshape(TALL, WIDE)
+    spread, most = sum_and_spread(lax.all_to_all(split, "width", 0, 0), note)
+    return lax.all_to_all(spread, "width", 0, 0).reshape(TALL, WIDE), most
 
 
 def local(activations, gradients, act_scale, grad_scale, counts, loss_mask):
@@ -310,10 +320,10 @@
     far_grads, near_grads = far_swap(grads), near_swap(grads)
     over_all = lax.all_to_all(over, "ex", 0, 0, tiled=True)
 
-    act_gram, _ = gram(acts, near_acts, far_acts, act_scale, parity, over, 1024, 300)
-    act_gram = sum_over_width(act_gram)
-    grad_gram, most = gram(grads, near_grads, far_grads, grad_scale, parity, over_all, PACK_TILE, 1)
+    act_gram = gram(acts, near_acts, far_acts, act_scale, parity, 300)
+    act_gram, most = sum_over_width(act_gram, over_all)
     crowded = most[0, 0] > 0.0
+    grad_gram = gram(grads, near_grads, far_grads, grad_scale, parity, 1)
     scores = finish(factor, grad_gram, act_gram, parity, (acts, near_acts, far_acts))
     mine = lax.all_to_all(scores, ("layer", "width"), 0, 0, tiled=True).sum(axis=0)
     ahead = from_behind(mine, "ex", 2)

time: 117 us -> 89.4 us (0.76)
  between operations: 13.6 us -> 0.26 us
  waiting for transfers between devices: 18.8 us -> 7.99 us
  Pallas kernels: 17.3 us -> 13.8 us
  blocking collectives: 39.4 us -> 40.7 us
  starting transfers between devices: 25 us -> 23.8 us
    all_to_all x1, waiting for transfers between devices: 6.73 us -> 0.01 us  [local(): over_all = lax.all_to_all(over, 'ex', 0, 0, tiled=True)]
    all_to_all x1, waiting for transfers between devices: 7.99 us -> 3.4 us  [sum_over_width(): return (lax.all_to_all(spread, 'width', 0, 0).reshape(TALL, WIDE), most)]
    pallas_call x2, Pallas kernels: 8.87 us -> 5.88 us  [gram(): pl.pallas_call(gram_kernel, grid=(features // tile,), in_specs=[block, bl...]
    all_to_all x1, starting transfers between devices: 6.68 us -> 4.36 us  [local(): over_all = lax.all_to_all(over, 'ex', 0, 0, tiled=True)]
    ppermute x2, starting transfers between devices: 8.64 us -> 10.4 us  [far_swap(): return lax.ppermute(value, 'ex', pairs)]
    all_to_all x1, blocking collectives: 20.3 us -> 21.5 us  [sum_over_width(): spread, most = sum_and_spread(lax.all_to_all(split, 'width', 0, 0), note)]
  transfers between devices with their start and end apart: 7 -> 7, of which waited for: 3 -> 2; matrix products, arithmetic and copies ran while one was open for 0% -> 0% of each run, Pallas kernels for 12% -> 12%
where the time goes in v2:
time: 89.4 us; the launch traced here: 88.8 us
  blocking collectives  40.7 us (46%)
  starting transfers between devices  23.8 us (27%)
  Pallas kernels  13.8 us (15%)
  waiting for transfers between devices  7.99 us (9%)
  local copies, waits for them, and re-layouts  2.01 us (2%)
    all_to_all x1, blocking collectives, sum_over_width(): spread, most = sum_and_spread(lax.all_to_all(split, 'width', 0, 0), note)  21.5 us
    all_to_all x1, blocking collectives, local(): lax.all_to_all(scores, ('layer', 'width'), 0, 0, tiled=True).sum(axis=0)  19.2 us
    ppermute x2, starting transfers between devices, far_swap(): return lax.ppermute(value, 'ex', pairs)  10.4 us
    pallas_call x2, Pallas kernels, gram(): pl.pallas_call(gram_kernel, grid=(features // tile,), in_specs=[block, bl...  5.88 us
    ppermute x1, waiting for transfers between devices, from_behind(): return lax.ppermute(value, axis, pairs)  4.58 us
    all_to_all x1, starting transfers between devices, local(): over_all = lax.all_to_all(over, 'ex', 0, 0, tiled=True)  4.36 us
    ppermute x2, starting transfers between devices, near_swap(): return lax.ppermute(value, 'ex', [(e, e ^ 1) for e in range(count)])  3.83 us
    pallas_call x1, Pallas kernels, pack_grads(): pl.pallas_call(pack_grads_kernel, grid=(features // TILE,), in_specs=[pl....  3.67 us
  transfers between devices with their start and end apart: 7, of which 2 were waited for; matrix products, arithmetic and copies ran while one was open for 0% of the time, Pallas kernels for 12%

profile of v2, /device:TPU:2, one launch (start us, length us, event | category | flops | bytes accessed | tf_op | source)
XLA Modules:
  0.0 88.8 jit_solution(5205119451748042718)
XLA Ops:
  0.0 0.7 copy-done
  0.7 0.7 copy-done.2
  1.3 2.0 %pack_acts.1 = (bf16[176,2176]{1,0:T(8,128)(2,1)S(1)}, bf16[176,256]{1,0:T(8,128)(2,1)S(1)}, f32[16,128]{1,0:T(8,128)}) custom-call(s32[8]{0:T(128)S(1)} %copy-done.2, s32[8,32]{1,0:T(8,128)S(1)} %copy-done, bf16[256,2048]{1,0:T(8,128)(2,1)} %bitcast.39), custom_call_target="tpu_custom_call" | custom-call | flops 184549376 | bytes 2097152 | tf_op jit(solution)/shard_map/pack_acts/pallas_call | solution.py:115
  3.4 1.9 %collective-permute-start.22 = (bf16[176,2176]{1,0:T(8,128)(2,1)S(1)}, bf16[176,2176]{1,0:T(8,128)(2,1)S(1)}, u32[]{:S(2)}, u32[]{:S(2)}) collective-permute-start(bf16[176,2176]{1,0:T(8,128)(2,1)S(1)} %get-tuple-element.54.own_ref.own_tag_ref), channel_id=1, source_target_pairs={{0,4},{4,0},{8,12},{12,8},{16,20},{20,16},{24,28},{28,24},{32,36},... | collective-permute-start | bytes 2297864 | tf_op jit(solution)/shard_map/ppermute | solution.py:296
  5.3 5.4 %collective-permute-start.21 = (bf16[176,2176]{1,0:T(8,128)(2,1)S(1)}, bf16[176,2176]{1,0:T(8,128)(2,1)S(1)}, u32[]{:S(2)}, u32[]{:S(2)}) collective-permute-start(bf16[176,2176]{1,0:T(8,128)(2,1)S(1)} %get-tuple-element.54.own_ref.own_tag_ref), channel_id=1, source_target_pairs={{0,56},{4,12},{8,0},{12,20},{16,8},{20,28},{24,16},{28,36},{32,24}... | collective-permute-start | bytes 2297864 | tf_op jit(solution)/shard_map/ppermute | solution.py:291
  10.7 4.4 %all-to-all-start.1 = ((f32[16,1,128]{2,1,0:T(1,128)}), f32[16,1,128]{2,1,0:T(1,128)}, u32[]{:S(2)}, u32[]{:S(2)}) async-start(f32[16,1,128]{2,1,0:T(1,128)} %bitcast.13), calls=%async_computation.1 | async-start | bytes 16384 | tf_op jit(solution)/shard_map/all_to_all | solution.py:321
  15.1 0.0 collective-permute-done.22.near_ref.after_ref.near_tag_ref
  15.1 0.0 copy-start.9
  15.1 3.7 %pack_grads.1.own_ref = bf16[176,7168]{1,0:T(8,128)(2,1)} custom-call(bf16[176,256]{1,0:T(8,128)(2,1)S(1)} %get-tuple-element.57.pick_ref, bf16[256,7168]{1,0:T(8,128)(2,1)} %bitcast.45, bf16[176,2176]{1,0:T(8,128)(2,1)S(1)} %collective-permute-done.22.near_ref.after_ref.near_tag_ref), custom_call_target="tpu_custom_call" | custom-call | flops 12918456320 | bytes 7340032 | tf_op jit(solution)/shard_map/pack_grads/pallas_call | solution.py:144
  18.8 5.0 %collective-permute-start.23 = (bf16[176,7168]{1,0:T(8,128)(2,1)}, bf16[176,7168]{1,0:T(8,128)(2,1)}, u32[]{:S(2)}, u32[]{:S(2)}) collective-permute-start(bf16[176,7168]{1,0:T(8,128)(2,1)} %pack_grads.1.own_ref), channel_id=1, source_target_pairs={{0,56},{4,12},{8,0},{12,20},{16,8},{20,28},{24,16},{28,36},{32,24}... | collective-permute-start | bytes 7569416 | tf_op jit(solution)/shard_map/ppermute | solution.py:291
  23.7 1.9 %collective-permute-start.24 = (bf16[176,7168]{1,0:T(8,128)(2,1)}, bf16[176,7168]{1,0:T(8,128)(2,1)}, u32[]{:S(2)}, u32[]{:S(2)}) collective-permute-start(bf16[176,7168]{1,0:T(8,128)(2,1)} %pack_grads.1.own_ref), channel_id=1, source_target_pairs={{0,4},{4,0},{8,12},{12,8},{16,20},{20,16},{24,28},{28,24},{32,36},... | collective-permute-start | bytes 7569416 | tf_op jit(solution)/shard_map/ppermute | solution.py:296
  25.7 0.0 collective-permute-done.21.far_ref.far_tag_ref
  25.7 0.0 copy-start.8
  25.7 1.0 %gram.2 = f32[192,640]{1,0:T(8,128)S(1)} custom-call(bf16[176,2176]{1,0:T(8,128)(2,1)S(1)} %collective-permute-done.21.far_ref.far_tag_ref, bf16[176,2176]{1,0:T(8,128)(2,1)S(1)} %collective-permute-done.22.near_ref.after_ref.near_tag_ref, bf16[176,2176]{1,0:T(8,128)(2,1)S(1)} %get-tuple-element.54.own_ref.own_tag_ref, f32[1,2048]{1,0:T(1,128)S(1)} %copy-done.9, ...), custom_call_target="tpu_custom_call" | custom-call | flops 241591910400 | bytes 2162688 | tf_op jit(solution)/shard_map/gram/pallas_call | solution.py:193
  26.7 0.0 all-to-all-done.1
  26.7 21.5 %all_to_all.30.parts_ref = f32[4,48,640]{2,1,0:T(8,128)S(1)} all-to-all(f32[4,48,640]{2,1,0:T(8,128)S(1)} %bitcast.36), channel_id=1, replica_groups=mesh['layer'=8,'ex'=16,'width'=4] {'width'}, dimensions={0} | all-to-all | bytes 983040 | tf_op jit(solution)/shard_map/all_to_all | solution.py:302
  48.2 1.4 %sum_and_spread.1 = (bf16[4,48,640]{2,1,0:T(8,128)(2,1)}, f32[1,128]{1,0:T(1,128)S(1)}) custom-call(f32[4,48,640]{2,1,0:T(8,128)S(1)} %all_to_all.30.parts_ref, f32[16,128]{1,0:T(8,128)} %bitcast.14.note_ref), custom_call_target="tpu_custom_call" | custom-call | tf_op jit(solution)/shard_map/sum_and_spread/pallas_call | solution.py:224
  49.7 3.4 %all-to-all-start.2 = ((bf16[4,48,640]{2,1,0:T(8,128)(2,1)}), bf16[4,48,640]{2,1,0:T(8,128)(2,1)S(1)}, u32[]{:S(2)}, u32[]{:S(2)}) async-start(bf16[4,48,640]{2,1,0:T(8,128)(2,1)} %get-tuple-element.58), calls=%async_computation.2 | async-start | bytes 491520 | tf_op jit(solution)/shard_map/all_to_all | solution.py:303
  53.1 0.0 copy-start.1
  53.1 0.0 copy-start.3
  53.1 4.9 %gram.3.grad_ref = f32[192,640]{1,0:T(8,128)S(1)} custom-call(bf16[176,7168]{1,0:T(8,128)(2,1)} %collective-permute-done.23.far_ref, bf16[176,7168]{1,0:T(8,128)(2,1)} %collective-permute-done.24.near_ref, bf16[176,7168]{1,0:T(8,128)(2,1)} %pack_grads.1.own_ref, f32[1,7168]{1,0:T(1,128)S(1)} %copy-done.8, s32[1]{0:T(128)} %bitcast.10.parity_ref), custom_call_target="tpu_custom_call" | custom-call | flops 2818572288 | bytes 7569408 | tf_op jit(solution)/shard_map/gram/pallas_call | solution.py:193
  58.0 3.4 %all-to-all-done.2 = bf16[4,48,640]{2,1,0:T(8,128)(2,1)S(1)} async-done(((bf16[4,48,640]{2,1,0:T(8,128)(2,1)}), bf16[4,48,640]{2,1,0:T(8,128)(2,1)S(1)}, u32[]{:S(2)}, u32[]{:S(2)}) %all-to-all-start.2) | async-done | bytes 245792 | tf_op jit(solution)/shard_map/all_to_all | solution.py:303
  61.4 0.7 finish.1
  62.1 19.2 %all_to_all.31 = f32[32,1,128]{2,1,0:T(1,128)S(1)} all-to-all(f32[32,1,128]{2,1,0:T(1,128)S(1)} %bitcast.37), channel_id=1, replica_groups=mesh['layer'=8,'ex'=16,'width'=4] {'layer','width'}, dimensions={0} | all-to-all | bytes 32768 | tf_op jit(solution)/shard_map/all_to_all | solution.py:328
  81.3 0.1 reduce_sum.36
  81.4 1.9 %collective-permute-start.25 = (f32[128]{0:T(128)S(1)}, f32[128]{0:T(128)S(1)}, u32[]{:S(2)}, u32[]{:S(2)}) collective-permute-start(f32[128]{0:T(128)S(1)} %reduce_sum.36), channel_id=1, source_target_pairs={{0,8},{4,12},{8,16},{12,20},{16,24},{20,28},{24,32},{28,36},{32,40... | collective-permute-start | bytes 1544 | tf_op jit(solution)/shard_map/ppermute | solution.py:28
  83.3 0.1 select_convert_fusion
  83.4 4.6 %collective-permute-done.25 = f32[128]{0:T(128)S(1)} collective-permute-done((f32[128]{0:T(128)S(1)}, f32[128]{0:T(128)S(1)}, u32[]{:S(2)}, u32[]{:S(2)}) %collective-permute-start.25) | collective-permute-done | bytes 544 | tf_op jit(solution)/shard_map/ppermute | solution.py:28
  88.0 0.2 conditional.1
  88.0 0.1 slice.19
  88.3 0.0 copy-start.10
  88.3 0.6 copy-done.10
  (10 shorter events, 0.0 us)
Async XLA Ops:
  0.0 0.7 copy-start
  0.7 0.7 copy-start.2
  3.4 11.7 %collective-permute-start.22 = (bf16[176,2176]{1,0:T(8,128)(2,1)S(1)}, bf16[176,2176]{1,0:T(8,128)(2,1)S(1)}, u32[]{:S(2)}, u32[]{:S(2)}) collective-permute-start(bf16[176,2176]{1,0:T(8,128)(2,1)S(1)} %get-tuple-element.54.own_ref.own_tag_ref), channel_id=1, source_target_pairs={{0,4},{4,0},{8,12},{12,8},{16,20},{20,16},{24,28},{28,24},{32,36},... | collective-permute-start | bytes 2297864 | tf_op jit(solution)/shard_map/ppermute | solution.py:296
  5.3 20.4 %collective-permute-start.21 = (bf16[176,2176]{1,0:T(8,128)(2,1)S(1)}, bf16[176,2176]{1,0:T(8,128)(2,1)S(1)}, u32[]{:S(2)}, u32[]{:S(2)}) collective-permute-start(bf16[176,2176]{1,0:T(8,128)(2,1)S(1)} %get-tuple-element.54.own_ref.own_tag_ref), channel_id=1, source_target_pairs={{0,56},{4,12},{8,0},{12,20},{16,8},{20,28},{24,16},{28,36},{32,24}... | collective-permute-start | bytes 2297864 | tf_op jit(solution)/shard_map/ppermute | solution.py:291
  10.7 16.0 %all-to-all-start.1 = ((f32[16,1,128]{2,1,0:T(1,128)}), f32[16,1,128]{2,1,0:T(1,128)}, u32[]{:S(2)}, u32[]{:S(2)}) async-start(f32[16,1,128]{2,1,0:T(1,128)} %bitcast.13), calls=%async_computation.1 | async-start | bytes 16384 | tf_op jit(solution)/shard_map/all_to_all | solution.py:321
  15.1 10.6 %copy-start.9 = (f32[1,2048]{1,0:T(1,128)S(1)}, f32[1,2048]{1,0:T(1,128)}, u32[]{:S(2)}) copy-start(f32[1,2048]{1,0:T(1,128)} %scale_ref.2) | copy-start | bytes 24580
  18.8 34.4 %collective-permute-start.23 = (bf16[176,7168]{1,0:T(8,128)(2,1)}, bf16[176,7168]{1,0:T(8,128)(2,1)}, u32[]{:S(2)}, u32[]{:S(2)}) collective-permute-start(bf16[176,7168]{1,0:T(8,128)(2,1)} %pack_grads.1.own_ref), channel_id=1, source_target_pairs={{0,56},{4,12},{8,0},{12,20},{16,8},{20,28},{24,16},{28,36},{32,24}... | collective-permute-start | bytes 7569416 | tf_op jit(solution)/shard_map/ppermute | solution.py:291
  23.7 29.4 %collective-permute-start.24 = (bf16[176,7168]{1,0:T(8,128)(2,1)}, bf16[176,7168]{1,0:T(8,128)(2,1)}, u32[]{:S(2)}, u32[]{:S(2)}) collective-permute-start(bf16[176,7168]{1,0:T(8,128)(2,1)} %pack_grads.1.own_ref), channel_id=1, source_target_pairs={{0,4},{4,0},{8,12},{12,8},{16,20},{20,16},{24,28},{28,24},{32,36},... | collective-permute-start | bytes 7569416 | tf_op jit(solution)/shard_map/ppermute | solution.py:296
  25.7 27.4 %copy-start.8 = (f32[1,7168]{1,0:T(1,128)S(1)}, f32[1,7168]{1,0:T(1,128)}, u32[]{:S(2)}) copy-start(f32[1,7168]{1,0:T(1,128)} %scale_ref.3) | copy-start | bytes 86020
  49.7 11.7 %all-to-all-start.2 = ((bf16[4,48,640]{2,1,0:T(8,128)(2,1)}), bf16[4,48,640]{2,1,0:T(8,128)(2,1)S(1)}, u32[]{:S(2)}, u32[]{:S(2)}) async-start(bf16[4,48,640]{2,1,0:T(8,128)(2,1)} %get-tuple-element.58), calls=%async_computation.2 | async-start | bytes 491520 | tf_op jit(solution)/shard_map/all_to_all | solution.py:303
  53.1 30.2 %copy-start.1 = (s32[8,32]{1,0:T(8,128)S(1)}, s32[8,32]{1,0:T(8,128)}, u32[]{:S(2)}) copy-start(s32[8,32]{1,0:T(8,128)} %mask_ref.1) | copy-start | bytes 3076
  53.1 30.2 %copy-start.3 = (s32[8]{0:T(128)S(1)}, s32[8]{0:T(128)}, u32[]{:S(2)}) copy-start(s32[8]{0:T(128)} %counts_ref.1) | copy-start | bytes 100
  81.4 6.6 %collective-permute-start.25 = (f32[128]{0:T(128)S(1)}, f32[128]{0:T(128)S(1)}, u32[]{:S(2)}, u32[]{:S(2)}) collective-permute-start(f32[128]{0:T(128)S(1)} %reduce_sum.36), channel_id=1, source_target_pairs={{0,8},{4,12},{8,16},{12,20},{16,24},{20,28},{24,32},{28,36},{32,40... | collective-permute-start | bytes 1544 | tf_op jit(solution)/shard_map/ppermute | solution.py:28
  88.3 0.6 copy-start.10

commit v3 on v2

--- a/solution.py
+++ b/solution.py
@@ -16,7 +16,7 @@
 OWN = 384
 WIDE = 640
 TAG = 128
-TILE = 3584
+PART = 1792
 BF16 = jnp.bfloat16
 F32 = jnp.float32
 VMEM_LIMIT = 24 * 1024 * 1024
@@ -85,7 +85,19 @@
     return jnp.sum(jnp.where(owner == row, wide, 0.0), axis=0, keepdims=True)
 
 
-def pack_acts_kernel(counts_ref, mask_ref, rows_ref, packed_ref, pick_ref, over_ref):
+def pack_acts_kernel(
+    counts_at, mask_at, rows_at, packed_ref, pick_ref, over_ref, counts_ref, mask_ref, rows_ref, done
+):
+    copies = [
+        pltpu.make_async_copy(source, target, done.at[place])
+        for place, (source, target) in enumerate(
+            ((counts_at, counts_ref), (mask_at, mask_ref), (rows_at, rows_ref))
+        )
+    ]
+    for copy in copies:
+        copy.start()
+    copies[0].wait()
+    copies[1].wait()
     features, rows = rows_ref.shape[1], rows_ref.shape[0]
     tok_slots = mask_ref.shape[1]
     weights = token_weights(counts_ref, mask_ref)
@@ -99,6 +111,7 @@
     pick_ref[...] = pick
     total = jnp.broadcast_to(jnp.sum(weights, axis=1, keepdims=True), over_ref.shape)
     over_ref[...] = jnp.where(total > CAP, 1.0, 0.0)
+    copies[2].wait()
     packed_ref[:, :features] = jnp.dot(pick, rows_ref[...], preferred_element_type=F32).astype(BF16)
     shape = (rows, TAG)
     example = lax.broadcasted_iota(jnp.int32, shape, 0) // tok_slots
@@ -114,13 +127,14 @@
     vmem = pl.BlockSpec(memory_space=pltpu.VMEM)
     return pl.pallas_call(
         pack_acts_kernel,
-        grid=(1,),
-        in_specs=[
-            pl.BlockSpec(memory_space=pltpu.SMEM),
-            pl.BlockSpec(mask.shape, lambda step: (0, 0)),
-            pl.BlockSpec(rows.shape, lambda step: (0, 0)),
-        ],
+        in_specs=[pl.BlockSpec(memory_space=pltpu.HBM)] * 3,
         out_specs=[vmem, vmem, vmem],
+        scratch_shapes=[
+            pltpu.SMEM(counts.shape, jnp.int32),
+            pltpu.VMEM(mask.shape, jnp.int32),
+            pltpu.VMEM(rows.shape, BF16),
+            pltpu.SemaphoreType.DMA((3,)),
+        ],
         out_shape=[
             jax.ShapeDtypeStruct((CAP, features + TAG), BF16),
             jax.ShapeDtypeStruct((CAP, count), BF16),
@@ -134,23 +148,54 @@
     )(counts, mask, rows)
 
 
-def pack_grads_kernel(pick_ref, rows_ref, after_ref, packed_ref):
-    del after_ref
-    packed_ref[...] = jnp.dot(pick_ref[...], rows_ref[...], preferred_element_type=F32).astype(BF16)
+def pack_grads_kernel(
+    pick_ref, rows_at, after_at, head_at, tail_at, rows_ref, packed_ref, came, left
+):
+    del after_at
+    head = head_at.shape[1]
+    firsts = range(0, rows_ref.shape[1], PART)
+    parts = [pl.ds(first, PART) for first in firsts]
+    loads = [
+        pltpu.make_async_copy(rows_at.at[:, part], rows_ref.at[:, part], came.at[place])
+        for place, part in enumerate(parts)
+    ]
+    targets = [
+        head_at.at[:, pl.ds(first, PART)] if first < head else tail_at.at[:, pl.ds(first - head, PART)]
+        for first in firsts
+    ]
+    stores = [
+        pltpu.make_async_copy(packed_ref.at[:, part], target, left.at[place])
+        for place, (part, target) in enumerate(zip(parts, targets))
+    ]
+    for load in loads:
+        load.start()
+    for part, load, store in zip(parts, loads, stores):
+        load.wait()
+        packed_ref[:, part] = jnp.dot(
+            pick_ref[...], rows_ref[:, part], preferred_element_type=F32
+        ).astype(BF16)
+        store.start()
+    for store in stores:
+        store.wait()
 
 
 def pack_grads(pick, rows, after):
     count, features = rows.shape
+    anywhere = pl.BlockSpec(memory_space=pl.ANY)
     return pl.pallas_call(
         pack_grads_kernel,
-        grid=(features // TILE,),
-        in_specs=[
-            pl.BlockSpec((CAP, count), lambda step: (0, 0)),
-            pl.BlockSpec((count, TILE), lambda step: (0, step)),
-            pl.BlockSpec(memory_space=pl.ANY),
-        ],
-        out_specs=pl.BlockSpec((CAP, TILE), lambda step: (0, step)),
-        out_shape=jax.ShapeDtypeStruct((CAP, features), BF16),
+        in_specs=[pl.BlockSpec(memory_space=pltpu.VMEM), anywhere, anywhere],
+        out_specs=[anywhere, anywhere],
+        out_shape=[
+            jax.ShapeDtypeStruct((CAP, features - PART), BF16),
+            jax.ShapeDtypeStruct((CAP, PART), BF16),
+        ],
+        scratch_shapes=[
+            pltpu.VMEM((count, features), BF16),
+            pltpu.VMEM((CAP, features), BF16),
+            pltpu.SemaphoreType.DMA((features // PART,)),
+            pltpu.SemaphoreType.DMA((features // PART,)),
+        ],
         compiler_params=pltpu.CompilerParams(vmem_limit_bytes=VMEM_LIMIT),
         cost_estimate=pl.CostEstimate(
             flops=40 * CAP * count * features, bytes_accessed=4 * count * features, transcendentals=0
@@ -161,59 +206,117 @@
 
 def gram_kernel(far_ref, near_ref, own_ref, scale_ref, parity_ref, gram_ref):
     contract = (((1,), (1,)), ((), ()))
-
-    @pl.when(pl.program_id(0) == 0)
-    def _():
-        gram_ref[...] = jnp.zeros_like(gram_ref)
+    features = scale_ref.shape[1]
+    gram_ref[...] = jnp.zeros_like(gram_ref)
+
+    def read(ref):
+        return ref[:, :features]
 
     def scaled(ref):
-        return (ref[...].astype(F32) * scale_ref[...]).astype(BF16)
-
-    def add(columns, left, right):
-        gram_ref[:CAP, columns] += lax.dot_general(left, right, contract, preferred_element_type=F32)
+        return (read(ref).astype(F32) * scale_ref[...]).astype(BF16)
+
+    def put(columns, left, right):
+        gram_ref[:CAP, columns] = lax.dot_general(
+            left, right, contract, preferred_element_type=F32
+        ).astype(BF16)
 
     pair, alone = slice(0, 2 * CAP), slice(OWN, OWN + CAP)
 
     @pl.when(parity_ref[0] == 1)
     def _():
         left = scaled(own_ref)
-        add(pair, left, jnp.concatenate([near_ref[...], far_ref[...]], axis=0))
-        add(alone, left, own_ref[...])
+        put(pair, left, jnp.concatenate([read(near_ref), read(far_ref)], axis=0))
+        put(alone, left, read(own_ref))
 
     @pl.when(parity_ref[0] == 0)
     def _():
-        add(pair, scaled(far_ref), jnp.concatenate([near_ref[...], own_ref[...]], axis=0))
-        add(alone, scaled(own_ref), own_ref[...])
-
-
-def gram(own, near, far, scale, parity, weight):
-    features = scale.shape[1]
-    tile = min(features, TILE)
-    block = pl.BlockSpec((CAP, tile), lambda step: (0, step))
+        put(pair, scaled(far_ref), jnp.concatenate([read(near_ref), read(own_ref)], axis=0))
+        put(alone, scaled(own_ref), read(own_ref))
+
+
+def gram(own, near, far, scale, parity):
+    vmem = pl.BlockSpec(memory_space=pltpu.VMEM)
     return pl.pallas_call(
         gram_kernel,
-        grid=(features // tile,),
-        in_specs=[
-            block,
-            block,
-            block,
-            pl.BlockSpec((1, tile), lambda step: (0, step)),
-            pl.BlockSpec(memory_space=pltpu.SMEM),
-        ],
-        out_specs=pl.BlockSpec((TALL, WIDE), lambda step: (0, 0)),
-        out_shape=jax.ShapeDtypeStruct((TALL, WIDE), F32),
+        in_specs=[vmem, vmem, vmem, vmem, pl.BlockSpec(memory_space=pltpu.SMEM)],
+        out_specs=vmem,
+        out_shape=jax.ShapeDtypeStruct((TALL, WIDE), BF16),
         compiler_params=pltpu.CompilerParams(vmem_limit_bytes=VMEM_LIMIT),
         cost_estimate=pl.CostEstimate(
-            flops=weight * 6 * 256 * 256 * features, bytes_accessed=6 * CAP * features, transcendentals=0
+            flops=1800 * 256 * 256 * scale.shape[1], bytes_accessed=6 * CAP * scale.shape[1], transcendentals=0
         ),
         name="gram",
     )(far, near, own, scale, parity)
 
 
+def add_grams(gram_ref, far_ref, near_ref, own_ref, scale_ref, parity_ref, part):
+    contract = (((1,), (1,)), ((), ()))
+
+    def scaled(ref):
+        return (ref[:, part].astype(F32) * scale_ref[:, part]).astype(BF16)
+
+    def add(columns, left, right):
+        gram_ref[:CAP, columns] += lax.dot_general(left, right, contract, preferred_element_type=F32)
+
+    pair, alone = slice(0, 2 * CAP), slice(OWN, OWN + CAP)
+
+    @pl.when(parity_ref[0] == 1)
+    def _():
+        left = scaled(own_ref)
+        add(pair, left, jnp.concatenate([near_ref[:, part], far_ref[:, part]], axis=0))
+        add(alone, left, own_ref[:, part])
+
+    @pl.when(parity_ref[0] == 0)
+    def _():
+        add(pair, scaled(far_ref), jnp.concatenate([near_ref[:, part], own_ref[:, part]], axis=0))
+        add(alone, scaled(own_ref), own_ref[:, part])
+
+
+def head_kernel(
+    far_at, near_at, own_at, scale_ref, parity_ref, gram_ref, far_ref, near_ref, own_ref, came
+):
+    parts = [pl.ds(first, PART) for first in range(0, own_at.shape[1], PART)]
+    blocks = ((far_at, far_ref), (near_at, near_ref), (own_at, own_ref))
+    loads = [
+        [
+            pltpu.make_async_copy(source.at[:, part], target.at[:, part], came.at[place, which])
+            for which, (source, target) in enumerate(blocks)
+        ]
+        for place, part in enumerate(parts)
+    ]
+    for row in loads:
+        for load in row:
+            load.start()
+    gram_ref[...] = jnp.zeros_like(gram_ref)
+    for part, row in zip(parts, loads):
+        for load in row:
+            load.wait()
+        add_grams(gram_ref, far_ref, near_ref, own_ref, scale_ref, parity_ref, part)
+
+
+def head_grams(own, near, far, scale, parity):
+    features = own.shape[1]
+    anywhere = pl.BlockSpec(memory_space=pl.ANY)
+    vmem = pl.BlockSpec(memory_space=pltpu.VMEM)
+    return pl.pallas_call(
+        head_kernel,
+        in_specs=[anywhere, anywhere, anywhere, vmem, pl.BlockSpec(memory_space=pltpu.SMEM)],
+        out_specs=vmem,
+        out_shape=jax.ShapeDtypeStruct((TALL, WIDE), F32),
+        scratch_shapes=[pltpu.VMEM((CAP, features), BF16)] * 3
+        + [pltpu.SemaphoreType.DMA((features // PART, 3))],
+        compiler_params=pltpu.CompilerParams(vmem_limit_bytes=VMEM_LIMIT),
+        cost_estimate=pl.CostEstimate(
+            flops=6 * 256 * 256 * features, bytes_accessed=6 * CAP * features, transcendentals=0
+        ),
+        name="head_grams",
+    )(far, near, own, scale, parity)
+
+
 def spread_kernel(parts_ref, note_ref, out_ref, said_ref):
-    total = parts_ref[0]
+    total = parts_ref[0].astype(F32)
     for part in range(1, parts_ref.shape[0]):
-        total = total + parts_ref[part]
+        total = total + parts_ref[part].astype(F32)
     rounded = total.astype(BF16)
     for part in range(out_ref.shape[0]):
         out_ref[part] = rounded
@@ -243,9 +346,12 @@
 
 
 def finish_kernel(
-    factor, grad_ref, act_ref, parity_ref, own_tag_ref, near_tag_ref, far_tag_ref, out_ref, tag_ref
+    factor, far_ref, near_ref, own_ref, scale_ref, head_ref, act_ref, parity_ref,
+    own_tag_ref, near_tag_ref, far_tag_ref, out_ref, gram_ref, tag_ref,
 ):
-    product = grad_ref[...] * act_ref[...].astype(F32)
+    gram_ref[...] = head_ref[...]
+    add_grams(gram_ref, far_ref, near_ref, own_ref, scale_ref, parity_ref, slice(None))
+    product = gram_ref[...] * act_ref[...].astype(F32)
     lane = lax.broadcasted_iota(jnp.int32, (CAP, TAG), 1) // 32
     odd = (parity_ref[0] == 1).astype(F32)
     own, near, far = (ref[...].astype(F32) for ref in (own_tag_ref, near_tag_ref, far_tag_ref))
@@ -269,20 +375,33 @@
     )
 
 
-def finish(factor, grad_gram, act_gram, parity, tags):
+def finish(factor, own, near, far, scale, head_gram, act_gram, parity, tags):
     tag_at = tags[0].shape[1] // TAG - 1
+    last = scale.shape[1] // PART - 1
+    block = pl.BlockSpec((CAP, PART), lambda step: (0, 0))
     whole = pl.BlockSpec((TALL, WIDE), lambda step: (0, 0))
     tag = pl.BlockSpec((CAP, TAG), lambda step: (0, tag_at))
     return pl.pallas_call(
         functools.partial(finish_kernel, factor),
         grid=(1,),
-        in_specs=[whole, whole, pl.BlockSpec(memory_space=pltpu.SMEM), tag, tag, tag],
+        in_specs=[
+            block,
+            block,
+            block,
+            pl.BlockSpec((1, PART), lambda step: (0, last)),
+            whole,
+            whole,
+            pl.BlockSpec(memory_space=pltpu.SMEM),
+            tag,
+            tag,
+            tag,
+        ],
         out_specs=pl.BlockSpec((32, TAG), lambda step: (0, 0)),
         out_shape=jax.ShapeDtypeStruct((32, TAG), F32),
-        scratch_shapes=[pltpu.VMEM((WIDE, TAG), BF16)],
+        scratch_shapes=[pltpu.VMEM((TALL, WIDE), F32), pltpu.VMEM((WIDE, TAG), BF16)],
         compiler_params=pltpu.CompilerParams(vmem_limit_bytes=VMEM_LIMIT),
         name="finish",
-    )(grad_gram, act_gram, parity, *tags)
+    )(far, near, own, scale, head_gram, act_gram, parity, *tags)
 
 
 def far_swap(value):
@@ -316,15 +435,19 @@
 
     acts, pick, over = pack_acts(counts, loss_mask, own_acts)
     far_acts, near_acts = far_swap(acts), near_swap(acts)
-    grads = pack_grads(pick, own_grads, near_acts)
-    far_grads, near_grads = far_swap(grads), near_swap(grads)
+    head, tail = pack_grads(pick, own_grads, near_acts)
+    far_head, far_tail = far_swap(head), far_swap(tail)
+    near_head, near_tail = near_swap(head), near_swap(tail)
+
     over_all = lax.all_to_all(over, "ex", 0, 0, tiled=True)
-
-    act_gram = gram(acts, near_acts, far_acts, act_scale, parity, 300)
+    act_gram = gram(acts, near_acts, far_acts, act_scale, parity)
     act_gram, most = sum_over_width(act_gram, over_all)
     crowded = most[0, 0] > 0.0
-    grad_gram = gram(grads, near_grads, far_grads, grad_scale, parity, 1)
-    scores = finish(factor, grad_gram, act_gram, parity, (acts, near_acts, far_acts))
+    head_gram = head_grams(head, near_head, far_head, grad_scale, parity)
+    scores = finish(
+        factor, tail, near_tail, far_tail, grad_scale, head_gram, act_gram, parity,
+        (acts, near_acts, far_acts),
+    )
     mine = lax.all_to_all(scores, ("layer", "width"), 0, 0, tiled=True).sum(axis=0)
     ahead = from_behind(mine, "ex", 2)
     place = lax.broadcasted_iota(jnp.int32, mine.shape, 0)

time: 89.4 us -> 85.9 us (0.961)
  blocking collectives: 40.7 us -> 19.2 us
  starting transfers between devices: 23.8 us -> 37.3 us
  local copies, waits for them, and re-layouts: 2.01 us -> 3.8 us
  waiting for transfers between devices: 7.99 us -> 9.77 us
    all_to_all x1 -> x0, blocking collectives: 21.5 us -> none  [sum_over_width(): spread, most = sum_and_spread(lax.all_to_all(split, 'width', 0, 0), note)]
    all_to_all x0 -> x1, starting transfers between devices: none -> 7.25 us  [sum_over_width(): spread, most = sum_and_spread(lax.all_to_all(split, 'width', 0, 0), note)]
    all_to_all x0 -> x1, waiting for transfers between devices: none -> 3.86 us  [sum_over_width(): spread, most = sum_and_spread(lax.all_to_all(split, 'width', 0, 0), note)]
    ppermute x2 -> x3, starting transfers between devices: 10.4 us -> 13.7 us  [far_swap(): return lax.ppermute(value, 'ex', pairs)]
    pallas_call x1, Pallas kernels: 0.73 us -> 2.77 us  [finish(): pl.pallas_call(functools.partial(finish_kernel, factor), grid=(1,), in_sp...]
    ppermute x2 -> x3, starting transfers between devices: 3.83 us -> 5.76 us  [near_swap(): return lax.ppermute(value, 'ex', [(e, e ^ 1) for e in range(count)])]
    unnamed x14 -> x18, local copies, waits for them, and re-layouts: 1.92 us -> 3.71 us
    all_to_all x1, waiting for transfers between devices: 3.4 us -> 2.09 us  [sum_over_width(): return (lax.all_to_all(spread, 'width', 0, 0).reshape(TALL, WIDE), most)]
  transfers between devices with their start and end apart: 7 -> 10, of which waited for: 2 -> 3; matrix products, arithmetic and copies ran while one was open for 0% -> 0% of each run, Pallas kernels for 12% -> 12%
where the time goes in v3:
time: 85.9 us; the launch traced here: 85.2 us
  starting transfers between devices  37.3 us (43%)
  blocking collectives  19.2 us (22%)
  Pallas kernels  14.6 us (17%)
  waiting for transfers between devices  9.77 us (11%)
  local copies, waits for them, and re-layouts  3.8 us (4%)
    all_to_all x1, blocking collectives, local(): lax.all_to_all(scores, ('layer', 'width'), 0, 0, tiled=True).sum(axis=0)  19.2 us
    ppermute x3, starting transfers between devices, far_swap(): return lax.ppermute(value, 'ex', pairs)  13.7 us
    all_to_all x1, starting transfers between devices, sum_over_width(): spread, most = sum_and_spread(lax.all_to_all(split, 'width', 0, 0), note)  7.25 us
    ppermute x3, starting transfers between devices, near_swap(): return lax.ppermute(value, 'ex', [(e, e ^ 1) for e in range(count)])  5.76 us
    all_to_all x1, starting transfers between devices, local(): over_all = lax.all_to_all(over, 'ex', 0, 0, tiled=True)  4.36 us
    all_to_all x1, waiting for transfers between devices, sum_over_width(): spread, most = sum_and_spread(lax.all_to_all(split, 'width', 0, 0), note)  3.86 us
    pallas_call x1, Pallas kernels, head_grams(): pl.pallas_call(head_kernel, in_specs=[anywhere, anywhere, anywhere, vmem,...  3.84 us
    ppermute x1, waiting for transfers between devices, from_behind(): return lax.ppermute(value, axis, pairs)  3.8 us
  transfers between devices with their start and end apart: 10, of which 3 were waited for; matrix products, arithmetic and copies ran while one was open for 0% of the time, Pallas kernels for 12%

profile of v3, /device:TPU:2, one launch (start us, length us, event | category | flops | bytes accessed | tf_op | source)
XLA Modules:
  0.0 85.2 jit_solution(8931634047409679784)
XLA Ops:
  0.0 0.7 copy-done.2
  0.7 0.7 copy-done.4
  1.3 1.8 %pack_acts.1 = (bf16[176,2176]{1,0:T(8,128)(2,1)S(1)}, bf16[176,256]{1,0:T(8,128)(2,1)S(1)}, f32[16,128]{1,0:T(8,128)}) custom-call(s32[8]{0:T(128)S(1)} %copy-done.4, s32[8,32]{1,0:T(8,128)S(1)} %copy-done.2, bf16[256,2048]{1,0:T(8,128)(2,1)} %bitcast.38), custom_call_target="tpu_custom_call" | custom-call | flops 184549376 | bytes 2097152 | tf_op jit(solution)/shard_map/pack_acts/pallas_call | solution.py:128
  3.2 1.9 %collective-permute-start.22 = (bf16[176,2176]{1,0:T(8,128)(2,1)S(1)}, bf16[176,2176]{1,0:T(8,128)(2,1)S(1)}, u32[]{:S(2)}, u32[]{:S(2)}) collective-permute-start(bf16[176,2176]{1,0:T(8,128)(2,1)S(1)} %get-tuple-element.56.own_ref.own_tag_ref), channel_id=1, source_target_pairs={{0,4},{4,0},{8,12},{12,8},{16,20},{20,16},{24,28},{28,24},{32,36},... | collective-permute-start | bytes 2297864 | tf_op jit(solution)/shard_map/ppermute | solution.py:415
  5.1 5.4 %collective-permute-start.21 = (bf16[176,2176]{1,0:T(8,128)(2,1)S(1)}, bf16[176,2176]{1,0:T(8,128)(2,1)S(1)}, u32[]{:S(2)}, u32[]{:S(2)}) collective-permute-start(bf16[176,2176]{1,0:T(8,128)(2,1)S(1)} %get-tuple-element.56.own_ref.own_tag_ref), channel_id=1, source_target_pairs={{0,56},{4,12},{8,0},{12,20},{16,8},{20,28},{24,16},{28,36},{32,24}... | collective-permute-start | bytes 2297864 | tf_op jit(solution)/shard_map/ppermute | solution.py:410
  10.5 4.4 %all-to-all-start.1 = ((f32[16,1,128]{2,1,0:T(1,128)}), f32[16,1,128]{2,1,0:T(1,128)}, u32[]{:S(2)}, u32[]{:S(2)}) async-start(f32[16,1,128]{2,1,0:T(1,128)} %bitcast.13), calls=%async_computation.1 | async-start | bytes 16384 | tf_op jit(solution)/shard_map/all_to_all | solution.py:442
  14.9 3.2 %pack_grads.1 = (bf16[176,5376]{1,0:T(8,128)(2,1)}, bf16[176,1792]{1,0:T(8,128)(2,1)S(1)}) custom-call(bf16[176,256]{1,0:T(8,128)(2,1)S(1)} %get-tuple-element.59.pick_ref, bf16[256,7168]{1,0:T(8,128)(2,1)} %bitcast.44, bf16[176,2176]{1,0:T(8,128)(2,1)S(1)} %collective-permute-done.22.near_ref.after_at.near_tag_ref), custom_call_target="tpu_custom_call" | custom-call | flops 12918456320 | bytes 7340032 | tf_op jit(solution)/shard_map/pack_grads/pallas_call | solution.py:185
  18.1 5.0 %collective-permute-start.25 = (bf16[176,5376]{1,0:T(8,128)(2,1)}, bf16[176,5376]{1,0:T(8,128)(2,1)}, u32[]{:S(2)}, u32[]{:S(2)}) collective-permute-start(bf16[176,5376]{1,0:T(8,128)(2,1)} %get-tuple-element.61.own_at), channel_id=1, source_target_pairs={{0,56},{4,12},{8,0},{12,20},{16,8},{20,28},{24,16},{28,36},{32,24}... | collective-permute-start | bytes 5677064 | tf_op jit(solution)/shard_map/ppermute | solution.py:410
  23.1 1.9 %collective-permute-start.26 = (bf16[176,5376]{1,0:T(8,128)(2,1)}, bf16[176,5376]{1,0:T(8,128)(2,1)}, u32[]{:S(2)}, u32[]{:S(2)}) collective-permute-start(bf16[176,5376]{1,0:T(8,128)(2,1)} %get-tuple-element.61.own_at), channel_id=1, source_target_pairs={{0,4},{4,0},{8,12},{12,8},{16,20},{20,16},{24,28},{28,24},{32,36},... | collective-permute-start | bytes 5677064 | tf_op jit(solution)/shard_map/ppermute | solution.py:415
  25.0 0.0 copy-start.10
  25.1 1.6 %gram.1 = bf16[192,640]{1,0:T(8,128)(2,1)} custom-call(bf16[176,2176]{1,0:T(8,128)(2,1)S(1)} %collective-permute-done.21.far_ref.far_tag_ref, bf16[176,2176]{1,0:T(8,128)(2,1)S(1)} %collective-permute-done.22.near_ref.after_at.near_tag_ref, bf16[176,2176]{1,0:T(8,128)(2,1)S(1)} %get-tuple-element.56.own_ref.own_tag_ref, f32[1,2048]{1,0:T(1,128)S(1)} %copy-done.11, ...), custom_call_target="tpu_custom_call" | custom-call | flops 241591910400 | bytes 2162688 | tf_op jit(solution)/shard_map/gram/pallas_call | solution.py:239
  26.6 7.2 %all-to-all-start = ((bf16[4,48,640]{2,1,0:T(8,128)(2,1)}), bf16[4,48,640]{2,1,0:T(8,128)(2,1)S(1)}, u32[]{:S(2)}, u32[]{:S(2)}) async-start(bf16[4,48,640]{2,1,0:T(8,128)(2,1)} %bitcast.11), calls=%async_computation | async-start | bytes 491520 | tf_op jit(solution)/shard_map/all_to_all | solution.py:421
  33.9 3.4 %collective-permute-start.23 = (bf16[176,1792]{1,0:T(8,128)(2,1)S(1)}, bf16[176,1792]{1,0:T(8,128)(2,1)}, u32[]{:S(2)}, u32[]{:S(2)}) collective-permute-start(bf16[176,1792]{1,0:T(8,128)(2,1)S(1)} %get-tuple-element.60.own_ref), channel_id=1, source_target_pairs={{0,56},{4,12},{8,0},{12,20},{16,8},{20,28},{24,16},{28,36},{32,24}... | collective-permute-start | bytes 1892360 | tf_op jit(solution)/shard_map/ppermute | solution.py:410
  37.3 1.9 %collective-permute-start.24 = (bf16[176,1792]{1,0:T(8,128)(2,1)S(1)}, bf16[176,1792]{1,0:T(8,128)(2,1)}, u32[]{:S(2)}, u32[]{:S(2)}) collective-permute-start(bf16[176,1792]{1,0:T(8,128)(2,1)S(1)} %get-tuple-element.60.own_ref), channel_id=1, source_target_pairs={{0,4},{4,0},{8,12},{12,8},{16,20},{20,16},{24,28},{28,24},{32,36},... | collective-permute-start | bytes 1892360 | tf_op jit(solution)/shard_map/ppermute | solution.py:415
  39.2 3.9 %all-to-all-done.parts_ref = bf16[4,48,640]{2,1,0:T(8,128)(2,1)S(1)} async-done(((bf16[4,48,640]{2,1,0:T(8,128)(2,1)}), bf16[4,48,640]{2,1,0:T(8,128)(2,1)S(1)}, u32[]{:S(2)}, u32[]{:S(2)}) %all-to-all-start) | async-done | bytes 245792 | tf_op jit(solution)/shard_map/all_to_all | solution.py:421
  43.0 1.4 %sum_and_spread.1 = (bf16[4,48,640]{2,1,0:T(8,128)(2,1)}, f32[1,128]{1,0:T(1,128)S(1)}) custom-call(bf16[4,48,640]{2,1,0:T(8,128)(2,1)S(1)} %all-to-all-done.parts_ref, f32[16,128]{1,0:T(8,128)} %bitcast.14.note_ref), custom_call_target="tpu_custom_call" | custom-call | tf_op jit(solution)/shard_map/sum_and_spread/pallas_call | solution.py:327
  44.5 3.4 %all-to-all-start.2 = ((bf16[4,48,640]{2,1,0:T(8,128)(2,1)}), bf16[4,48,640]{2,1,0:T(8,128)(2,1)S(1)}, u32[]{:S(2)}, u32[]{:S(2)}) async-start(bf16[4,48,640]{2,1,0:T(8,128)(2,1)} %get-tuple-element.62), calls=%async_computation.2 | async-start | bytes 491520 | tf_op jit(solution)/shard_map/all_to_all | solution.py:422
  47.9 0.0 copy-start.3
  47.9 3.8 %head_grams.1.head_ref = f32[192,640]{1,0:T(8,128)S(1)} custom-call(bf16[176,5376]{1,0:T(8,128)(2,1)} %collective-permute-done.25.far_at, bf16[176,5376]{1,0:T(8,128)(2,1)} %collective-permute-done.26.near_at, bf16[176,5376]{1,0:T(8,128)(2,1)} %get-tuple-element.61.own_at, f32[1,7168]{1,0:T(1,128)S(1)} %copy-done.10, s32[1]{0:T(128)} %bitcast.10.parity_ref), custom_call_target="tpu_custom_call" | custom-call | flops 2113929216 | bytes 5677056 | tf_op jit(solution)/shard_map/head_grams/pallas_call | solution.py:301
  51.8 0.8 copy-done
  52.5 2.1 %all-to-all-done.2 = bf16[4,48,640]{2,1,0:T(8,128)(2,1)S(1)} async-done(((bf16[4,48,640]{2,1,0:T(8,128)(2,1)}), bf16[4,48,640]{2,1,0:T(8,128)(2,1)S(1)}, u32[]{:S(2)}, u32[]{:S(2)}) %all-to-all-start.2) | async-done | bytes 245792 | tf_op jit(solution)/shard_map/all_to_all | solution.py:422
  54.6 1.0 %copy-done.1 = f32[192,640]{1,0:T(8,128)S(1)} copy-done((f32[192,640]{1,0:T(8,128)S(1)}, f32[192,640]{1,0:T(8,128)}, u32[]{:S(2)}) %copy-start.1) | copy-done | bytes 491544
  55.7 2.8 %finish.1 = f32[32,128]{1,0:T(8,128)S(1)} custom-call(bf16[176,1792]{1,0:T(8,128)(2,1)} %collective-permute-done.23.far_ref, bf16[176,1792]{1,0:T(8,128)(2,1)} %collective-permute-done.24.near_ref, bf16[176,1792]{1,0:T(8,128)(2,1)S(1)} %get-tuple-element.60.own_ref, f32[1,7168]{1,0:T(1,128)S(1)} %copy-done.10, f32[192,640]{1,0:T(8,128)S(1)} %copy-done.1, ...), custom_call_target="tpu_custom_call" | custom-call | tf_op jit(solution)/shard_map/finish/pallas_call | solution.py:384
  58.4 19.2 %all_to_all.30 = f32[32,1,128]{2,1,0:T(1,128)S(1)} all-to-all(f32[32,1,128]{2,1,0:T(1,128)S(1)} %bitcast.36), channel_id=1, replica_groups=mesh['layer'=8,'ex'=16,'width'=4] {'layer','width'}, dimensions={0} | all-to-all | bytes 32768 | tf_op jit(solution)/shard_map/all_to_all | solution.py:451
  77.6 0.1 reduce_sum.36
  77.6 2.8 %collective-permute-start.27 = (f32[128]{0:T(128)S(1)}, f32[128]{0:T(128)S(1)}, u32[]{:S(2)}, u32[]{:S(2)}) collective-permute-start(f32[128]{0:T(128)S(1)} %reduce_sum.36), channel_id=1, source_target_pairs={{0,8},{4,12},{8,16},{12,20},{16,24},{20,28},{24,32},{28,36},{32,40... | collective-permute-start | bytes 1544 | tf_op jit(solution)/shard_map/ppermute | solution.py:28
  80.4 0.1 select_convert_fusion
  80.6 3.8 %collective-permute-done.27 = f32[128]{0:T(128)S(1)} collective-permute-done((f32[128]{0:T(128)S(1)}, f32[128]{0:T(128)S(1)}, u32[]{:S(2)}, u32[]{:S(2)}) %collective-permute-start.27) | collective-permute-done | bytes 544 | tf_op jit(solution)/shard_map/ppermute | solution.py:28
  84.4 0.2 conditional.1
  84.4 0.1 slice.19
  84.6 0.0 copy-start.12
  84.6 0.6 copy-done.12
  (19 shorter events, 0.0 us)
Async XLA Ops:
  0.0 0.7 copy-start.2
  0.7 0.7 copy-start.4
  3.2 11.7 %collective-permute-start.22 = (bf16[176,2176]{1,0:T(8,128)(2,1)S(1)}, bf16[176,2176]{1,0:T(8,128)(2,1)S(1)}, u32[]{:S(2)}, u32[]{:S(2)}) collective-permute-start(bf16[176,2176]{1,0:T(8,128)(2,1)S(1)} %get-tuple-element.56.own_ref.own_tag_ref), channel_id=1, source_target_pairs={{0,4},{4,0},{8,12},{12,8},{16,20},{20,16},{24,28},{28,24},{32,36},... | collective-permute-start | bytes 2297864 | tf_op jit(solution)/shard_map/ppermute | solution.py:415
  5.1 19.9 %collective-permute-start.21 = (bf16[176,2176]{1,0:T(8,128)(2,1)S(1)}, bf16[176,2176]{1,0:T(8,128)(2,1)S(1)}, u32[]{:S(2)}, u32[]{:S(2)}) collective-permute-start(bf16[176,2176]{1,0:T(8,128)(2,1)S(1)} %get-tuple-element.56.own_ref.own_tag_ref), channel_id=1, source_target_pairs={{0,56},{4,12},{8,0},{12,20},{16,8},{20,28},{24,16},{28,36},{32,24}... | collective-permute-start | bytes 2297864 | tf_op jit(solution)/shard_map/ppermute | solution.py:410
  10.5 16.1 %all-to-all-start.1 = ((f32[16,1,128]{2,1,0:T(1,128)}), f32[16,1,128]{2,1,0:T(1,128)}, u32[]{:S(2)}, u32[]{:S(2)}) async-start(f32[16,1,128]{2,1,0:T(1,128)} %bitcast.13), calls=%async_computation.1 | async-start | bytes 16384 | tf_op jit(solution)/shard_map/all_to_all | solution.py:442
  14.9 10.1 %copy-start.11 = (f32[1,2048]{1,0:T(1,128)S(1)}, f32[1,2048]{1,0:T(1,128)}, u32[]{:S(2)}) copy-start(f32[1,2048]{1,0:T(1,128)} %scale_ref.3) | copy-start | bytes 24580
  18.1 29.8 %collective-permute-start.25 = (bf16[176,5376]{1,0:T(8,128)(2,1)}, bf16[176,5376]{1,0:T(8,128)(2,1)}, u32[]{:S(2)}, u32[]{:S(2)}) collective-permute-start(bf16[176,5376]{1,0:T(8,128)(2,1)} %get-tuple-element.61.own_at), channel_id=1, source_target_pairs={{0,56},{4,12},{8,0},{12,20},{16,8},{20,28},{24,16},{28,36},{32,24}... | collective-permute-start | bytes 5677064 | tf_op jit(solution)/shard_map/ppermute | solution.py:410
  23.1 24.8 %collective-permute-start.26 = (bf16[176,5376]{1,0:T(8,128)(2,1)}, bf16[176,5376]{1,0:T(8,128)(2,1)}, u32[]{:S(2)}, u32[]{:S(2)}) collective-permute-start(bf16[176,5376]{1,0:T(8,128)(2,1)} %get-tuple-element.61.own_at), channel_id=1, source_target_pairs={{0,4},{4,0},{8,12},{12,8},{16,20},{20,16},{24,28},{28,24},{32,36},... | collective-permute-start | bytes 5677064 | tf_op jit(solution)/shard_map/ppermute | solution.py:415
  25.0 22.9 %copy-start.10 = (f32[1,7168]{1,0:T(1,128)S(1)}, f32[1,7168]{1,0:T(1,128)}, u32[]{:S(2)}) copy-start(f32[1,7168]{1,0:T(1,128)} %scale_ref.5) | copy-start | bytes 86020
  26.6 16.4 %all-to-all-start = ((bf16[4,48,640]{2,1,0:T(8,128)(2,1)}), bf16[4,48,640]{2,1,0:T(8,128)(2,1)S(1)}, u32[]{:S(2)}, u32[]{:S(2)}) async-start(bf16[4,48,640]{2,1,0:T(8,128)(2,1)} %bitcast.11), calls=%async_computation | async-start | bytes 491520 | tf_op jit(solution)/shard_map/all_to_all | solution.py:421
  33.9 18.6 %collective-permute-start.23 = (bf16[176,1792]{1,0:T(8,128)(2,1)S(1)}, bf16[176,1792]{1,0:T(8,128)(2,1)}, u32[]{:S(2)}, u32[]{:S(2)}) collective-permute-start(bf16[176,1792]{1,0:T(8,128)(2,1)S(1)} %get-tuple-element.60.own_ref), channel_id=1, source_target_pairs={{0,56},{4,12},{8,0},{12,20},{16,8},{20,28},{24,16},{28,36},{32,24}... | collective-permute-start | bytes 1892360 | tf_op jit(solution)/shard_map/ppermute | solution.py:410
  37.3 15.3 %collective-permute-start.24 = (bf16[176,1792]{1,0:T(8,128)(2,1)S(1)}, bf16[176,1792]{1,0:T(8,128)(2,1)}, u32[]{:S(2)}, u32[]{:S(2)}) collective-permute-start(bf16[176,1792]{1,0:T(8,128)(2,1)S(1)} %get-tuple-element.60.own_ref), channel_id=1, source_target_pairs={{0,4},{4,0},{8,12},{12,8},{16,20},{20,16},{24,28},{28,24},{32,36},... | collective-permute-start | bytes 1892360 | tf_op jit(solution)/shard_map/ppermute | solution.py:415
  44.5 10.2 %all-to-all-start.2 = ((bf16[4,48,640]{2,1,0:T(8,128)(2,1)}), bf16[4,48,640]{2,1,0:T(8,128)(2,1)S(1)}, u32[]{:S(2)}, u32[]{:S(2)}) async-start(bf16[4,48,640]{2,1,0:T(8,128)(2,1)} %get-tuple-element.62), calls=%async_computation.2 | async-start | bytes 491520 | tf_op jit(solution)/shard_map/all_to_all | solution.py:422
  47.9 32.5 %copy-start.3 = (s32[8,32]{1,0:T(8,128)S(1)}, s32[8,32]{1,0:T(8,128)}, u32[]{:S(2)}) copy-start(s32[8,32]{1,0:T(8,128)} %mask_at.1) | copy-start | bytes 3076
  51.8 0.8 copy-start
  52.5 27.9 %copy-start.5 = (s32[8]{0:T(128)S(1)}, s32[8]{0:T(128)}, u32[]{:S(2)}) copy-start(s32[8]{0:T(128)} %counts_at.1) | copy-start | bytes 100
  54.6 1.0 %copy-start.1 = (f32[192,640]{1,0:T(8,128)S(1)}, f32[192,640]{1,0:T(8,128)}, u32[]{:S(2)}) copy-start(f32[192,640]{1,0:T(8,128)} %copy-done) | copy-start | bytes 1474564
  77.6 6.7 %collective-permute-start.27 = (f32[128]{0:T(128)S(1)}, f32[128]{0:T(128)S(1)}, u32[]{:S(2)}, u32[]{:S(2)}) collective-permute-start(f32[128]{0:T(128)S(1)} %reduce_sum.36), channel_id=1, source_target_pairs={{0,8},{4,12},{8,16},{12,20},{16,24},{20,28},{24,32},{28,36},{32,40... | collective-permute-start | bytes 1544 | tf_op jit(solution)/shard_map/ppermute | solution.py:28
  84.6 0.6 copy-start.12

commit v4 on v3

--- a/solution.py
+++ b/solution.py
@@ -11,7 +11,7 @@
 D = 8192
 FF = 28672
 HOPS = 2
-CAP = 176
+CAPS = (176, 192)
 TALL = 192
 OWN = 384
 WIDE = 640
@@ -46,19 +46,21 @@
     factor = 1.0 / (math.sqrt(D * FF) * tok_slots)
     contract = (((1,), (1,)), ((), ()))
 
-    def pair_scores(partner):
-        move_acts, move_grads, move_weight = partner
-        act_gram = lax.dot_general(stat_acts, move_acts, contract, preferred_element_type=F32)
-        grad_gram = lax.dot_general(stat_grads, move_grads, contract, preferred_element_type=F32)
-        act_gram, grad_gram = butterfly_sum(act_gram, "width"), butterfly_sum(grad_gram, "width")
-        product = act_gram * grad_gram * weight_rows[:, None] * move_weight.astype(F32)[None, :]
-        return product.reshape(ex_local, tok_slots, ex_local, tok_slots).sum(axis=(1, 3)) * factor
-
     partner = (own_acts, own_grads, weight_rows.astype(BF16))
-    scores = [pair_scores(partner)]
-    for distance in range(HOPS):
-        partner = tuple(from_behind(value, "ex", 1) for value in partner)
-        scores.append(pair_scores(partner))
+    grams, move_weights = [], []
+    for distance in range(HOPS + 1):
+        if distance:
+            partner = tuple(from_behind(value, "ex", 1) for value in partner)
+        for stat, move in ((stat_acts, partner[0]), (stat_grads, partner[1])):
+            grams.append(lax.dot_general(stat, move, contract, preferred_element_type=F32))
+        move_weights.append(partner[2].astype(F32))
+    grams = butterfly_sum(jnp.stack(grams), "width")
+    scores = []
+    for distance, move_weight in enumerate(move_weights):
+        product = grams[2 * distance] * grams[2 * distance + 1]
+        product = product * weight_rows[:, None] * move_weight[None, :]
+        product = product.reshape(ex_local, tok_slots, ex_local, tok_slots)
+        scores.append(product.sum(axis=(1, 3)) * factor)
     local_ex = lax.broadcasted_iota(jnp.int32, (ex_local, ex_local), 0)
     column_ex = lax.broadcasted_iota(jnp.int32, (ex_local, ex_local), 1)
     scores[0] = scores[0] * (local_ex != column_ex).astype(F32)
@@ -86,7 +88,7 @@
 
 
 def pack_acts_kernel(
-    counts_at, mask_at, rows_at, packed_ref, pick_ref, over_ref, counts_ref, mask_ref, rows_ref, done
+    counts_at, mask_at, rows_at, packed_ref, pick_ref, many_ref, counts_ref, mask_ref, rows_ref, done
 ):
     copies = [
         pltpu.make_async_copy(source, target, done.at[place])
@@ -106,11 +108,11 @@
     ramp = jnp.where(before <= upto, 1.0, 0.0).astype(BF16)
     lifted = jnp.broadcast_to(weights, (16, rows)).astype(BF16)
     rank = jnp.dot(lifted, ramp, preferred_element_type=F32)[0:1]
-    slot = lax.broadcasted_iota(jnp.int32, (CAP, rows), 0).astype(F32) + 1.0
+    slot = lax.broadcasted_iota(jnp.int32, (pick_ref.shape[0], rows), 0).astype(F32) + 1.0
     pick = (jnp.where(slot == rank, 1.0, 0.0) * weights).astype(BF16)
     pick_ref[...] = pick
-    total = jnp.broadcast_to(jnp.sum(weights, axis=1, keepdims=True), over_ref.shape)
-    over_ref[...] = jnp.where(total > CAP, 1.0, 0.0)
+    total = jnp.broadcast_to(jnp.sum(weights, axis=1, keepdims=True), many_ref.shape)
+    many_ref[...] = total
     copies[2].wait()
     packed_ref[:, :features] = jnp.dot(pick, rows_ref[...], preferred_element_type=F32).astype(BF16)
     shape = (rows, TAG)
@@ -122,7 +124,7 @@
     packed_ref[:, features:] = jnp.dot(pick, tags, preferred_element_type=F32).astype(BF16)
 
 
-def pack_acts(counts, mask, rows):
+def pack_acts(counts, mask, rows, cap):
     count, features = rows.shape
     vmem = pl.BlockSpec(memory_space=pltpu.VMEM)
     return pl.pallas_call(
@@ -136,13 +138,13 @@
             pltpu.SemaphoreType.DMA((3,)),
         ],
         out_shape=[
-            jax.ShapeDtypeStruct((CAP, features + TAG), BF16),
-            jax.ShapeDtypeStruct((CAP, count), BF16),
+            jax.ShapeDtypeStruct((cap, features + TAG), BF16),
+            jax.ShapeDtypeStruct((cap, count), BF16),
             jax.ShapeDtypeStruct((16, TAG), F32),
         ],
         compiler_params=pltpu.CompilerParams(vmem_limit_bytes=VMEM_LIMIT),
         cost_estimate=pl.CostEstimate(
-            flops=2 * CAP * count * features, bytes_accessed=4 * count * features, transcendentals=0
+            flops=2 * cap * count * features, bytes_accessed=4 * count * features, transcendentals=0
         ),
         name="pack_acts",
     )(counts, mask, rows)
@@ -181,24 +183,25 @@
 
 def pack_grads(pick, rows, after):
     count, features = rows.shape
+    cap = pick.shape[0]
     anywhere = pl.BlockSpec(memory_space=pl.ANY)
     return pl.pallas_call(
         pack_grads_kernel,
         in_specs=[pl.BlockSpec(memory_space=pltpu.VMEM), anywhere, anywhere],
         out_specs=[anywhere, anywhere],
         out_shape=[
-            jax.ShapeDtypeStruct((CAP, features - PART), BF16),
-            jax.ShapeDtypeStruct((CAP, PART), BF16),
+            jax.ShapeDtypeStruct((cap, features - PART), BF16),
+            jax.ShapeDtypeStruct((cap, PART), BF16),
         ],
         scratch_shapes=[
             pltpu.VMEM((count, features), BF16),
-            pltpu.VMEM((CAP, features), BF16),
+            pltpu.VMEM((cap, features), BF16),
             pltpu.SemaphoreType.DMA((features // PART,)),
             pltpu.SemaphoreType.DMA((features // PART,)),
         ],
         compiler_params=pltpu.CompilerParams(vmem_limit_bytes=VMEM_LIMIT),
         cost_estimate=pl.CostEstimate(
-            flops=40 * CAP * count * features, bytes_accessed=4 * count * features, transcendentals=0
+            flops=40 * cap * count * features, bytes_accessed=4 * count * features, transcendentals=0
         ),
         name="pack_grads",
     )(pick, rows, after)
@@ -207,6 +210,7 @@
 def gram_kernel(far_ref, near_ref, own_ref, scale_ref, parity_ref, gram_ref):
     contract = (((1,), (1,)), ((), ()))
     features = scale_ref.shape[1]
+    cap = own_ref.shape[0]
     gram_ref[...] = jnp.zeros_like(gram_ref)
 
     def read(ref):
@@ -216,11 +220,11 @@
         return (read(ref).astype(F32) * scale_ref[...]).astype(BF16)
 
     def put(columns, left, right):
-        gram_ref[:CAP, columns] = lax.dot_general(
+        gram_ref[:cap, columns] = lax.dot_general(
             left, right, contract, preferred_element_type=F32
         ).astype(BF16)
 
-    pair, alone = slice(0, 2 * CAP), slice(OWN, OWN + CAP)
+    pair, alone = slice(0, 2 * cap), slice(OWN, OWN + cap)
 
     @pl.when(parity_ref[0] == 1)
     def _():
@@ -243,7 +247,7 @@
         out_shape=jax.ShapeDtypeStruct((TALL, WIDE), BF16),
         compiler_params=pltpu.CompilerParams(vmem_limit_bytes=VMEM_LIMIT),
         cost_estimate=pl.CostEstimate(
-            flops=1800 * 256 * 256 * scale.shape[1], bytes_accessed=6 * CAP * scale.shape[1], transcendentals=0
+            flops=1800 * 256 * 256 * scale.shape[1], bytes_accessed=6 * own.shape[0] * scale.shape[1], transcendentals=0
         ),
         name="gram",
     )(far, near, own, scale, parity)
@@ -251,14 +255,15 @@
 
 def add_grams(gram_ref, far_ref, near_ref, own_ref, scale_ref, parity_ref, part):
     contract = (((1,), (1,)), ((), ()))
+    cap = own_ref.shape[0]
 
     def scaled(ref):
         return (ref[:, part].astype(F32) * scale_ref[:, part]).astype(BF16)
 
     def add(columns, left, right):
-        gram_ref[:CAP, columns] += lax.dot_general(left, right, contract, preferred_element_type=F32)
-
-    pair, alone = slice(0, 2 * CAP), slice(OWN, OWN + CAP)
+        gram_ref[:cap, columns] += lax.dot_general(left, right, contract, preferred_element_type=F32)
+
+    pair, alone = slice(0, 2 * cap), slice(OWN, OWN + cap)
 
     @pl.when(parity_ref[0] == 1)
     def _():
@@ -295,7 +300,7 @@
 
 
 def head_grams(own, near, far, scale, parity):
-    features = own.shape[1]
+    cap, features = own.shape
     anywhere = pl.BlockSpec(memory_space=pl.ANY)
     vmem = pl.BlockSpec(memory_space=pltpu.VMEM)
     return pl.pallas_call(
@@ -303,11 +308,11 @@
         in_specs=[anywhere, anywhere, anywhere, vmem, pl.BlockSpec(memory_space=pltpu.SMEM)],
         out_specs=vmem,
         out_shape=jax.ShapeDtypeStruct((TALL, WIDE), F32),
-        scratch_shapes=[pltpu.VMEM((CAP, features), BF16)] * 3
+        scratch_shapes=[pltpu.VMEM((cap, features), BF16)] * 3
         + [pltpu.SemaphoreType.DMA((features // PART, 3))],
         compiler_params=pltpu.CompilerParams(vmem_limit_bytes=VMEM_LIMIT),
         cost_estimate=pl.CostEstimate(
-            flops=6 * 256 * 256 * features, bytes_accessed=6 * CAP * features, transcendentals=0
+            flops=6 * 256 * 256 * features, bytes_accessed=6 * cap * features, transcendentals=0
         ),
         name="head_grams",
     )(far, near, own, scale, parity)
@@ -349,19 +354,20 @@
     factor, far_ref, near_ref, own_ref, scale_ref, head_ref, act_ref, parity_ref,
     own_tag_ref, near_tag_ref, far_tag_ref, out_ref, gram_ref, tag_ref,
 ):
+    cap = own_ref.shape[0]
     gram_ref[...] = head_ref[...]
     add_grams(gram_ref, far_ref, near_ref, own_ref, scale_ref, parity_ref, slice(None))
     product = gram_ref[...] * act_ref[...].astype(F32)
-    lane = lax.broadcasted_iota(jnp.int32, (CAP, TAG), 1) // 32
+    lane = lax.broadcasted_iota(jnp.int32, (cap, TAG), 1) // 32
     odd = (parity_ref[0] == 1).astype(F32)
     own, near, far = (ref[...].astype(F32) for ref in (own_tag_ref, near_tag_ref, far_tag_ref))
     last = odd * far + (1.0 - odd) * own
     left = odd * own + (1.0 - odd) * far
     tag_ref[...] = jnp.zeros_like(tag_ref)
-    tag_ref[:CAP] = jnp.where(lane == 1, near, 0.0).astype(BF16)
-    tag_ref[CAP : 2 * CAP] = jnp.where(lane == 2, last, 0.0).astype(BF16)
-    tag_ref[OWN : OWN + CAP] = jnp.where(lane == 3, own, 0.0).astype(BF16)
-    by_column = exact_dot(product, tag_ref[...], (((1,), (0,)), ((), ())))[:CAP]
+    tag_ref[:cap] = jnp.where(lane == 1, near, 0.0).astype(BF16)
+    tag_ref[cap : 2 * cap] = jnp.where(lane == 2, last, 0.0).astype(BF16)
+    tag_ref[OWN : OWN + cap] = jnp.where(lane == 3, own, 0.0).astype(BF16)
+    by_column = exact_dot(product, tag_ref[...], (((1,), (0,)), ((), ())))[:cap]
     by_row = (((0,), (0,)), ((), ()))
     pairs = exact_dot(by_column, left.astype(BF16), by_row)
     selves = exact_dot(by_column, own.astype(BF16), by_row)
@@ -378,9 +384,10 @@
 def finish(factor, own, near, far, scale, head_gram, act_gram, parity, tags):
     tag_at = tags[0].shape[1] // TAG - 1
     last = scale.shape[1] // PART - 1
-    block = pl.BlockSpec((CAP, PART), lambda step: (0, 0))
+    cap = own.shape[0]
+    block = pl.BlockSpec((cap, PART), lambda step: (0, 0))
     whole = pl.BlockSpec((TALL, WIDE), lambda step: (0, 0))
-    tag = pl.BlockSpec((CAP, TAG), lambda step: (0, tag_at))
+    tag = pl.BlockSpec((cap, TAG), lambda step: (0, tag_at))
     return pl.pallas_call(
         functools.partial(finish_kernel, factor),
         grid=(1,),
@@ -422,27 +429,23 @@
     return lax.all_to_all(spread, "width", 0, 0).reshape(TALL, WIDE), most
 
 
-def local(activations, gradients, act_scale, grad_scale, counts, loss_mask):
+def packed(cap, activations, gradients, act_scale, grad_scale, counts, loss_mask):
     ex_local, tok_slots = loss_mask.shape
     row_count = ex_local * tok_slots
     own_acts = activations[0].reshape(row_count, -1)
     own_grads = gradients[0].reshape(row_count, -1)
-    positions = lax.broadcasted_iota(jnp.int32, (ex_local, tok_slots), 1)
-    token_weight = (positions < counts[:, None]).astype(jnp.int32) * loss_mask
-    weight_rows = token_weight.astype(F32).reshape(row_count)
     parity = (lax.axis_index("ex") % 2).astype(jnp.int32).reshape(1)
     factor = 1.0 / (math.sqrt(D * FF) * tok_slots)
 
-    acts, pick, over = pack_acts(counts, loss_mask, own_acts)
-    far_acts, near_acts = far_swap(acts), near_swap(acts)
+    acts, pick, many = pack_acts(counts, loss_mask, own_acts, cap)
+    near_acts, far_acts = near_swap(acts), far_swap(acts)
     head, tail = pack_grads(pick, own_grads, near_acts)
     far_head, far_tail = far_swap(head), far_swap(tail)
     near_head, near_tail = near_swap(head), near_swap(tail)
 
-    over_all = lax.all_to_all(over, "ex", 0, 0, tiled=True)
+    many = lax.all_to_all(many, "ex", 0, 0, tiled=True)
     act_gram = gram(acts, near_acts, far_acts, act_scale, parity)
-    act_gram, most = sum_over_width(act_gram, over_all)
-    crowded = most[0, 0] > 0.0
+    act_gram, most = sum_over_width(act_gram, many)
     head_gram = head_grams(head, near_head, far_head, grad_scale, parity)
     scores = finish(
         factor, tail, near_tail, far_tail, grad_scale, head_gram, act_gram, parity,
@@ -452,12 +455,24 @@
     ahead = from_behind(mine, "ex", 2)
     place = lax.broadcasted_iota(jnp.int32, mine.shape, 0)
     kept = jnp.where((place < 8) | (parity[0] == 1), mine, ahead)
-    quick = kept[: 8 * (HOPS + 1)].reshape(HOPS + 1, ex_local, 1)
-    return lax.cond(
-        crowded,
-        lambda: plain(activations, gradients, act_scale, grad_scale, weight_rows, tok_slots),
-        lambda: quick,
-    )
+    return kept[: 8 * (HOPS + 1)].reshape(HOPS + 1, ex_local, 1), most[0, 0]
+
+
+def local(activations, gradients, act_scale, grad_scale, counts, loss_mask):
+    args = (activations, gradients, act_scale, grad_scale, counts, loss_mask)
+    quick, most = packed(CAPS[0], *args)
+
+    def whole():
+        ex_local, tok_slots = loss_mask.shape
+        positions = lax.broadcasted_iota(jnp.int32, (ex_local, tok_slots), 1)
+        token_weight = (positions < counts[:, None]).astype(jnp.int32) * loss_mask
+        weight_rows = token_weight.astype(F32).reshape(ex_local * tok_slots)
+        return plain(activations, gradients, act_scale, grad_scale, weight_rows, tok_slots)
+
+    def larger():
+        return lax.cond(most > CAPS[1], whole, lambda: packed(CAPS[1], *args)[0])
+
+    return lax.cond(most > CAPS[0], larger, lambda: quick)
 
 
 def solution(mesh):

time: 85.9 us -> 84.6 us (0.985)
  local copies, waits for them, and re-layouts: 3.8 us -> 2.46 us
    unnamed x18 -> x10, local copies, waits for them, and re-layouts: 3.71 us -> 2.37 us
where the time goes in v4:
time: 84.6 us; the launch traced here: 83.9 us
  starting transfers between devices  37.3 us (44%)
  blocking collectives  19.2 us (23%)
  Pallas kernels  14.7 us (17%)
  waiting for transfers between devices  9.86 us (12%)
  local copies, waits for them, and re-layouts  2.46 us (3%)
    all_to_all x1, blocking collectives, packed(): lax.all_to_all(scores, ('layer', 'width'), 0, 0, tiled=True).sum(axis=0)  19.2 us
    ppermute x3, starting transfers between devices, far_swap(): return lax.ppermute(value, 'ex', pairs)  13.7 us
    all_to_all x1, starting transfers between devices, sum_over_width(): spread, most = sum_and_spread(lax.all_to_all(split, 'width', 0, 0), note)  7.26 us
    ppermute x3, starting transfers between devices, near_swap(): return lax.ppermute(value, 'ex', [(e, e ^ 1) for e in range(count)])  5.76 us
    all_to_all x1, starting transfers between devices, packed(): many = lax.all_to_all(many, 'ex', 0, 0, tiled=True)  4.36 us
    ppermute x1, waiting for transfers between devices, from_behind(): return lax.ppermute(value, axis, pairs)  3.89 us
    all_to_all x1, waiting for transfers between devices, sum_over_width(): spread, most = sum_and_spread(lax.all_to_all(split, 'width', 0, 0), note)  3.86 us
    pallas_call x1, Pallas kernels, head_grams(): pl.pallas_call(head_kernel, in_specs=[anywhere, anywhere, anywhere, vmem,...  3.84 us
  transfers between devices with their start and end apart: 10, of which 3 were waited for; matrix products, arithmetic and copies ran while one was open for 0% of the time, Pallas kernels for 12%

profile of v4, /device:TPU:2, one launch (start us, length us, event | category | flops | bytes accessed | tf_op | source)
XLA Modules:
  0.0 83.9 jit_solution(3875590794426193904)
XLA Ops:
  0.0 1.9 %pack_acts.3 = (bf16[176,2176]{1,0:T(8,128)(2,1)S(1)}, bf16[176,256]{1,0:T(8,128)(2,1)S(1)}, f32[16,128]{1,0:T(8,128)}) custom-call(s32[8]{0:T(128)} %counts_at.1, s32[8,32]{1,0:T(8,128)} %mask_at.1, bf16[256,2048]{1,0:T(8,128)(2,1)} %bitcast.77), custom_call_target="tpu_custom_call" | custom-call | flops 184549376 | bytes 2097152 | tf_op jit(solution)/shard_map/pack_acts/pallas_call | solution.py:130
  1.9 1.9 %collective-permute-start.19 = (bf16[176,2176]{1,0:T(8,128)(2,1)S(1)}, bf16[176,2176]{1,0:T(8,128)(2,1)S(1)}, u32[]{:S(2)}, u32[]{:S(2)}) collective-permute-start(bf16[176,2176]{1,0:T(8,128)(2,1)S(1)} %get-tuple-element.104.own_ref.own_tag_ref), channel_id=1, source_target_pairs={{0,4},{4,0},{8,12},{12,8},{16,20},{20,16},{24,28},{28,24},{32,36},... | collective-permute-start | bytes 2297864 | tf_op jit(solution)/shard_map/ppermute | solution.py:422
  3.8 5.4 %collective-permute-start.18 = (bf16[176,2176]{1,0:T(8,128)(2,1)S(1)}, bf16[176,2176]{1,0:T(8,128)(2,1)S(1)}, u32[]{:S(2)}, u32[]{:S(2)}) collective-permute-start(bf16[176,2176]{1,0:T(8,128)(2,1)S(1)} %get-tuple-element.104.own_ref.own_tag_ref), channel_id=1, source_target_pairs={{0,56},{4,12},{8,0},{12,20},{16,8},{20,28},{24,16},{28,36},{32,24}... | collective-permute-start | bytes 2297864 | tf_op jit(solution)/shard_map/ppermute | solution.py:417
  9.2 4.4 %all-to-all-start.5 = ((f32[16,1,128]{2,1,0:T(1,128)}), f32[16,1,128]{2,1,0:T(1,128)}, u32[]{:S(2)}, u32[]{:S(2)}) async-start(f32[16,1,128]{2,1,0:T(1,128)} %bitcast.29), calls=%async_computation.5 | async-start | bytes 16384 | tf_op jit(solution)/shard_map/all_to_all | solution.py:446
  13.6 0.0 collective-permute-done.19.near_ref.after_at.near_tag_ref
  13.6 0.0 copy-start.12
  13.6 3.2 %pack_grads.3 = (bf16[176,5376]{1,0:T(8,128)(2,1)}, bf16[176,1792]{1,0:T(8,128)(2,1)S(1)}) custom-call(bf16[176,256]{1,0:T(8,128)(2,1)S(1)} %get-tuple-element.107.pick_ref, bf16[256,7168]{1,0:T(8,128)(2,1)} %bitcast.84, bf16[176,2176]{1,0:T(8,128)(2,1)S(1)} %collective-permute-done.19.near_ref.after_at.near_tag_ref), custom_call_target="tpu_custom_call" | custom-call | flops 12918456320 | bytes 7340032 | tf_op jit(solution)/shard_map/pack_grads/pallas_call | solution.py:188
  16.8 5.0 %collective-permute-start.22 = (bf16[176,5376]{1,0:T(8,128)(2,1)}, bf16[176,5376]{1,0:T(8,128)(2,1)}, u32[]{:S(2)}, u32[]{:S(2)}) collective-permute-start(bf16[176,5376]{1,0:T(8,128)(2,1)} %get-tuple-element.109.own_at), channel_id=1, source_target_pairs={{0,56},{4,12},{8,0},{12,20},{16,8},{20,28},{24,16},{28,36},{32,24}... | collective-permute-start | bytes 5677064 | tf_op jit(solution)/shard_map/ppermute | solution.py:417
  21.8 1.9 %collective-permute-start.23 = (bf16[176,5376]{1,0:T(8,128)(2,1)}, bf16[176,5376]{1,0:T(8,128)(2,1)}, u32[]{:S(2)}, u32[]{:S(2)}) collective-permute-start(bf16[176,5376]{1,0:T(8,128)(2,1)} %get-tuple-element.109.own_at), channel_id=1, source_target_pairs={{0,4},{4,0},{8,12},{12,8},{16,20},{20,16},{24,28},{28,24},{32,36},... | collective-permute-start | bytes 5677064 | tf_op jit(solution)/shard_map/ppermute | solution.py:422
  23.7 0.0 collective-permute-done.18.far_ref.far_tag_ref
  23.8 0.0 copy-start.8
  23.8 1.6 %gram.3 = bf16[192,640]{1,0:T(8,128)(2,1)} custom-call(bf16[176,2176]{1,0:T(8,128)(2,1)S(1)} %collective-permute-done.18.far_ref.far_tag_ref, bf16[176,2176]{1,0:T(8,128)(2,1)S(1)} %collective-permute-done.19.near_ref.after_at.near_tag_ref, bf16[176,2176]{1,0:T(8,128)(2,1)S(1)} %get-tuple-element.104.own_ref.own_tag_ref, f32[1,2048]{1,0:T(1,128)S(1)} %copy-done.12, ...), custom_call_target="tpu_custom_call" | custom-call | flops 241591910400 | bytes 2162688 | tf_op jit(solution)/shard_map/gram/pallas_call | solution.py:243
  25.4 0.0 all-to-all-done.5
  25.4 7.3 %all-to-all-start.4 = ((bf16[4,48,640]{2,1,0:T(8,128)(2,1)}), bf16[4,48,640]{2,1,0:T(8,128)(2,1)S(1)}, u32[]{:S(2)}, u32[]{:S(2)}) async-start(bf16[4,48,640]{2,1,0:T(8,128)(2,1)} %bitcast.27), calls=%async_computation.4 | async-start | bytes 491520 | tf_op jit(solution)/shard_map/all_to_all | solution.py:428
  32.6 3.4 %collective-permute-start.20 = (bf16[176,1792]{1,0:T(8,128)(2,1)S(1)}, bf16[176,1792]{1,0:T(8,128)(2,1)}, u32[]{:S(2)}, u32[]{:S(2)}) collective-permute-start(bf16[176,1792]{1,0:T(8,128)(2,1)S(1)} %get-tuple-element.108.own_ref), channel_id=1, source_target_pairs={{0,56},{4,12},{8,0},{12,20},{16,8},{20,28},{24,16},{28,36},{32,24}... | collective-permute-start | bytes 1892360 | tf_op jit(solution)/shard_map/ppermute | solution.py:417
  36.0 1.9 %collective-permute-start.21 = (bf16[176,1792]{1,0:T(8,128)(2,1)S(1)}, bf16[176,1792]{1,0:T(8,128)(2,1)}, u32[]{:S(2)}, u32[]{:S(2)}) collective-permute-start(bf16[176,1792]{1,0:T(8,128)(2,1)S(1)} %get-tuple-element.108.own_ref), channel_id=1, source_target_pairs={{0,4},{4,0},{8,12},{12,8},{16,20},{20,16},{24,28},{28,24},{32,36},... | collective-permute-start | bytes 1892360 | tf_op jit(solution)/shard_map/ppermute | solution.py:422
  37.9 3.9 %all-to-all-done.4.parts_ref = bf16[4,48,640]{2,1,0:T(8,128)(2,1)S(1)} async-done(((bf16[4,48,640]{2,1,0:T(8,128)(2,1)}), bf16[4,48,640]{2,1,0:T(8,128)(2,1)S(1)}, u32[]{:S(2)}, u32[]{:S(2)}) %all-to-all-start.4) | async-done | bytes 245792 | tf_op jit(solution)/shard_map/all_to_all | solution.py:428
  41.8 1.4 %sum_and_spread.3 = (bf16[4,48,640]{2,1,0:T(8,128)(2,1)}, f32[1,128]{1,0:T(1,128)S(1)}) custom-call(bf16[4,48,640]{2,1,0:T(8,128)(2,1)S(1)} %all-to-all-done.4.parts_ref, f32[16,128]{1,0:T(8,128)} %bitcast.30.note_ref), custom_call_target="tpu_custom_call" | custom-call | tf_op jit(solution)/shard_map/sum_and_spread/pallas_call | solution.py:332
  43.2 3.4 %all-to-all-start.6 = ((bf16[4,48,640]{2,1,0:T(8,128)(2,1)}), bf16[4,48,640]{2,1,0:T(8,128)(2,1)S(1)}, u32[]{:S(2)}, u32[]{:S(2)}) async-start(bf16[4,48,640]{2,1,0:T(8,128)(2,1)} %get-tuple-element.110), calls=%async_computation.6 | async-start | bytes 491520 | tf_op jit(solution)/shard_map/all_to_all | solution.py:429
  46.7 3.8 %head_grams.3.head_ref = f32[192,640]{1,0:T(8,128)S(1)} custom-call(bf16[176,5376]{1,0:T(8,128)(2,1)} %collective-permute-done.22.far_at, bf16[176,5376]{1,0:T(8,128)(2,1)} %collective-permute-done.23.near_at, bf16[176,5376]{1,0:T(8,128)(2,1)} %get-tuple-element.109.own_at, f32[1,7168]{1,0:T(1,128)S(1)} %copy-done.8, s32[1]{0:T(128)} %bitcast.26.parity_ref), custom_call_target="tpu_custom_call" | custom-call | flops 2113929216 | bytes 5677056 | tf_op jit(solution)/shard_map/head_grams/pallas_call | solution.py:306
  50.5 0.8 copy-done
  51.3 2.1 %all-to-all-done.6 = bf16[4,48,640]{2,1,0:T(8,128)(2,1)S(1)} async-done(((bf16[4,48,640]{2,1,0:T(8,128)(2,1)}), bf16[4,48,640]{2,1,0:T(8,128)(2,1)S(1)}, u32[]{:S(2)}, u32[]{:S(2)}) %all-to-all-start.6) | async-done | bytes 245792 | tf_op jit(solution)/shard_map/all_to_all | solution.py:429
  53.4 1.0 %copy-done.1 = f32[192,640]{1,0:T(8,128)S(1)} copy-done((f32[192,640]{1,0:T(8,128)S(1)}, f32[192,640]{1,0:T(8,128)}, u32[]{:S(2)}) %copy-start.1) | copy-done | bytes 491544
  54.4 2.8 %finish.3 = f32[32,128]{1,0:T(8,128)S(1)} custom-call(bf16[176,1792]{1,0:T(8,128)(2,1)} %collective-permute-done.20.far_ref, bf16[176,1792]{1,0:T(8,128)(2,1)} %collective-permute-done.21.near_ref, bf16[176,1792]{1,0:T(8,128)(2,1)S(1)} %get-tuple-element.108.own_ref, f32[1,7168]{1,0:T(1,128)S(1)} %copy-done.8, f32[192,640]{1,0:T(8,128)S(1)} %copy-done.1, ...), custom_call_target="tpu_custom_call" | custom-call | tf_op jit(solution)/shard_map/finish/pallas_call | solution.py:391
  57.2 19.2 %all_to_all.54 = f32[32,1,128]{2,1,0:T(1,128)S(1)} all-to-all(f32[32,1,128]{2,1,0:T(1,128)S(1)} %bitcast.75), channel_id=1, replica_groups=mesh['layer'=8,'ex'=16,'width'=4] {'layer','width'}, dimensions={0} | all-to-all | bytes 32768 | tf_op jit(solution)/shard_map/all_to_all | solution.py:454
  76.3 0.1 reduce_sum.45
  76.4 2.8 %collective-permute-start.24 = (f32[128]{0:T(128)S(1)}, f32[128]{0:T(128)S(1)}, u32[]{:S(2)}, u32[]{:S(2)}) collective-permute-start(f32[128]{0:T(128)S(1)} %reduce_sum.45), channel_id=1, source_target_pairs={{0,8},{4,12},{8,16},{12,20},{16,24},{20,28},{24,32},{28,36},{32,40... | collective-permute-start | bytes 1544 | tf_op jit(solution)/shard_map/ppermute | solution.py:28
  79.2 3.9 %collective-permute-done.24 = f32[128]{0:T(128)S(1)} collective-permute-done((f32[128]{0:T(128)S(1)}, f32[128]{0:T(128)S(1)}, u32[]{:S(2)}, u32[]{:S(2)}) %collective-permute-start.24) | collective-permute-done | bytes 544 | tf_op jit(solution)/shard_map/ppermute | solution.py:28
  83.1 0.2 conditional.2
  83.1 0.1 slice.50
  83.3 0.0 copy-start.16
  83.3 0.6 copy-done.16
  (10 shorter events, 0.0 us)
Async XLA Ops:
  1.9 11.7 %collective-permute-start.19 = (bf16[176,2176]{1,0:T(8,128)(2,1)S(1)}, bf16[176,2176]{1,0:T(8,128)(2,1)S(1)}, u32[]{:S(2)}, u32[]{:S(2)}) collective-permute-start(bf16[176,2176]{1,0:T(8,128)(2,1)S(1)} %get-tuple-element.104.own_ref.own_tag_ref), channel_id=1, source_target_pairs={{0,4},{4,0},{8,12},{12,8},{16,20},{20,16},{24,28},{28,24},{32,36},... | collective-permute-start | bytes 2297864 | tf_op jit(solution)/shard_map/ppermute | solution.py:422
  3.8 20.0 %collective-permute-start.18 = (bf16[176,2176]{1,0:T(8,128)(2,1)S(1)}, bf16[176,2176]{1,0:T(8,128)(2,1)S(1)}, u32[]{:S(2)}, u32[]{:S(2)}) collective-permute-start(bf16[176,2176]{1,0:T(8,128)(2,1)S(1)} %get-tuple-element.104.own_ref.own_tag_ref), channel_id=1, source_target_pairs={{0,56},{4,12},{8,0},{12,20},{16,8},{20,28},{24,16},{28,36},{32,24}... | collective-permute-start | bytes 2297864 | tf_op jit(solution)/shard_map/ppermute | solution.py:417
  9.2 16.2 %all-to-all-start.5 = ((f32[16,1,128]{2,1,0:T(1,128)}), f32[16,1,128]{2,1,0:T(1,128)}, u32[]{:S(2)}, u32[]{:S(2)}) async-start(f32[16,1,128]{2,1,0:T(1,128)} %bitcast.29), calls=%async_computation.5 | async-start | bytes 16384 | tf_op jit(solution)/shard_map/all_to_all | solution.py:446
  13.6 10.2 %copy-start.12 = (f32[1,2048]{1,0:T(1,128)S(1)}, f32[1,2048]{1,0:T(1,128)}, u32[]{:S(2)}) copy-start(f32[1,2048]{1,0:T(1,128)} %scale_ref.3) | copy-start | bytes 24580
  16.8 29.8 %collective-permute-start.22 = (bf16[176,5376]{1,0:T(8,128)(2,1)}, bf16[176,5376]{1,0:T(8,128)(2,1)}, u32[]{:S(2)}, u32[]{:S(2)}) collective-permute-start(bf16[176,5376]{1,0:T(8,128)(2,1)} %get-tuple-element.109.own_at), channel_id=1, source_target_pairs={{0,56},{4,12},{8,0},{12,20},{16,8},{20,28},{24,16},{28,36},{32,24}... | collective-permute-start | bytes 5677064 | tf_op jit(solution)/shard_map/ppermute | solution.py:417
  21.8 24.8 %collective-permute-start.23 = (bf16[176,5376]{1,0:T(8,128)(2,1)}, bf16[176,5376]{1,0:T(8,128)(2,1)}, u32[]{:S(2)}, u32[]{:S(2)}) collective-permute-start(bf16[176,5376]{1,0:T(8,128)(2,1)} %get-tuple-element.109.own_at), channel_id=1, source_target_pairs={{0,4},{4,0},{8,12},{12,8},{16,20},{20,16},{24,28},{28,24},{32,36},... | collective-permute-start | bytes 5677064 | tf_op jit(solution)/shard_map/ppermute | solution.py:422
  23.8 22.9 %copy-start.8 = (f32[1,7168]{1,0:T(1,128)S(1)}, f32[1,7168]{1,0:T(1,128)}, u32[]{:S(2)}) copy-start(f32[1,7168]{1,0:T(1,128)} %scale_ref.5) | copy-start | bytes 86020
  25.4 16.4 %all-to-all-start.4 = ((bf16[4,48,640]{2,1,0:T(8,128)(2,1)}), bf16[4,48,640]{2,1,0:T(8,128)(2,1)S(1)}, u32[]{:S(2)}, u32[]{:S(2)}) async-start(bf16[4,48,640]{2,1,0:T(8,128)(2,1)} %bitcast.27), calls=%async_computation.4 | async-start | bytes 491520 | tf_op jit(solution)/shard_map/all_to_all | solution.py:428
  32.6 18.7 %collective-permute-start.20 = (bf16[176,1792]{1,0:T(8,128)(2,1)S(1)}, bf16[176,1792]{1,0:T(8,128)(2,1)}, u32[]{:S(2)}, u32[]{:S(2)}) collective-permute-start(bf16[176,1792]{1,0:T(8,128)(2,1)S(1)} %get-tuple-element.108.own_ref), channel_id=1, source_target_pairs={{0,56},{4,12},{8,0},{12,20},{16,8},{20,28},{24,16},{28,36},{32,24}... | collective-permute-start | bytes 1892360 | tf_op jit(solution)/shard_map/ppermute | solution.py:417
  36.0 15.3 %collective-permute-start.21 = (bf16[176,1792]{1,0:T(8,128)(2,1)S(1)}, bf16[176,1792]{1,0:T(8,128)(2,1)}, u32[]{:S(2)}, u32[]{:S(2)}) collective-permute-start(bf16[176,1792]{1,0:T(8,128)(2,1)S(1)} %get-tuple-element.108.own_ref), channel_id=1, source_target_pairs={{0,4},{4,0},{8,12},{12,8},{16,20},{20,16},{24,28},{28,24},{32,36},... | collective-permute-start | bytes 1892360 | tf_op jit(solution)/shard_map/ppermute | solution.py:422
  43.2 10.2 %all-to-all-start.6 = ((bf16[4,48,640]{2,1,0:T(8,128)(2,1)}), bf16[4,48,640]{2,1,0:T(8,128)(2,1)S(1)}, u32[]{:S(2)}, u32[]{:S(2)}) async-start(bf16[4,48,640]{2,1,0:T(8,128)(2,1)} %get-tuple-element.110), calls=%async_computation.6 | async-start | bytes 491520 | tf_op jit(solution)/shard_map/all_to_all | solution.py:429
  50.5 0.8 copy-start
  53.4 1.0 %copy-start.1 = (f32[192,640]{1,0:T(8,128)S(1)}, f32[192,640]{1,0:T(8,128)}, u32[]{:S(2)}) copy-start(f32[192,640]{1,0:T(8,128)} %copy-done) | copy-start | bytes 1474564
  76.4 6.7 %collective-permute-start.24 = (f32[128]{0:T(128)S(1)}, f32[128]{0:T(128)S(1)}, u32[]{:S(2)}, u32[]{:S(2)}) collective-permute-start(f32[128]{0:T(128)S(1)} %reduce_sum.45), channel_id=1, source_target_pairs={{0,8},{4,12},{8,16},{12,20},{16,24},{20,28},{24,32},{28,36},{32,40... | collective-permute-start | bytes 1544 | tf_op jit(solution)/shard_map/ppermute | solution.py:28
  83.3 0.6 copy-start.16

commit v5 on v4

--- a/solution.py
+++ b/solution.py
@@ -452,7 +452,8 @@
         (acts, near_acts, far_acts),
     )
     mine = lax.all_to_all(scores, ("layer", "width"), 0, 0, tiled=True).sum(axis=0)
-    ahead = from_behind(mine, "ex", 2)
+    count = lax.axis_size("ex")
+    ahead = lax.ppermute(mine, "ex", [(e, (e + 2) % count) for e in range(0, count, 2)])
     place = lax.broadcasted_iota(jnp.int32, mine.shape, 0)
     kept = jnp.where((place < 8) | (parity[0] == 1), mine, ahead)
     return kept[: 8 * (HOPS + 1)].reshape(HOPS + 1, ex_local, 1), most[0, 0]

time: 84.6 us -> 84.6 us (level)
  no operation moved by 1% of the time
where the time goes in v5:
time: 84.6 us; the launch traced here: 83.9 us
  starting transfers between devices  37.3 us (44%)
  blocking collectives  19.2 us (23%)
  Pallas kernels  14.7 us (17%)
  waiting for transfers between devices  9.86 us (12%)
  local copies, waits for them, and re-layouts  2.46 us (3%)
    all_to_all x1, blocking collectives, packed(): lax.all_to_all(scores, ('layer', 'width'), 0, 0, tiled=True).sum(axis=0)  19.2 us
    ppermute x3, starting transfers between devices, far_swap(): return lax.ppermute(value, 'ex', pairs)  13.7 us
    all_to_all x1, starting transfers between devices, sum_over_width(): spread, most = sum_and_spread(lax.all_to_all(split, 'width', 0, 0), note)  7.26 us
    ppermute x3, starting transfers between devices, near_swap(): return lax.ppermute(value, 'ex', [(e, e ^ 1) for e in range(count)])  5.76 us
    all_to_all x1, starting transfers between devices, packed(): many = lax.all_to_all(many, 'ex', 0, 0, tiled=True)  4.36 us
    ppermute x1, waiting for transfers between devices, packed(): lax.ppermute(mine, 'ex', [(e, (e + 2) % count) for e in range(0, count, 2)])  3.89 us
    all_to_all x1, waiting for transfers between devices, sum_over_width(): spread, most = sum_and_spread(lax.all_to_all(split, 'width', 0, 0), note)  3.86 us
    pallas_call x1, Pallas kernels, head_grams(): pl.pallas_call(head_kernel, in_specs=[anywhere, anywhere, anywhere, vmem,...  3.84 us
  transfers between devices with their start and end apart: 10, of which 3 were waited for; matrix products, arithmetic and copies ran while one was open for 0% of the time, Pallas kernels for 12%

profile of v5, /device:TPU:2, one launch (start us, length us, event | category | flops | bytes accessed | tf_op | source)
XLA Modules:
  0.0 83.9 jit_solution(365354274006598838)
XLA Ops:
  0.0 1.9 %pack_acts.3 = (bf16[176,2176]{1,0:T(8,128)(2,1)S(1)}, bf16[176,256]{1,0:T(8,128)(2,1)S(1)}, f32[16,128]{1,0:T(8,128)}) custom-call(s32[8]{0:T(128)} %counts_at.1, s32[8,32]{1,0:T(8,128)} %mask_at.1, bf16[256,2048]{1,0:T(8,128)(2,1)} %bitcast.77), custom_call_target="tpu_custom_call" | custom-call | flops 184549376 | bytes 2097152 | tf_op jit(solution)/shard_map/pack_acts/pallas_call | solution.py:130
  1.9 1.9 %collective-permute-start.19 = (bf16[176,2176]{1,0:T(8,128)(2,1)S(1)}, bf16[176,2176]{1,0:T(8,128)(2,1)S(1)}, u32[]{:S(2)}, u32[]{:S(2)}) collective-permute-start(bf16[176,2176]{1,0:T(8,128)(2,1)S(1)} %get-tuple-element.104.own_ref.own_tag_ref), channel_id=1, source_target_pairs={{0,4},{4,0},{8,12},{12,8},{16,20},{20,16},{24,28},{28,24},{32,36},... | collective-permute-start | bytes 2297864 | tf_op jit(solution)/shard_map/ppermute | solution.py:422
  3.8 5.4 %collective-permute-start.18 = (bf16[176,2176]{1,0:T(8,128)(2,1)S(1)}, bf16[176,2176]{1,0:T(8,128)(2,1)S(1)}, u32[]{:S(2)}, u32[]{:S(2)}) collective-permute-start(bf16[176,2176]{1,0:T(8,128)(2,1)S(1)} %get-tuple-element.104.own_ref.own_tag_ref), channel_id=1, source_target_pairs={{0,56},{4,12},{8,0},{12,20},{16,8},{20,28},{24,16},{28,36},{32,24}... | collective-permute-start | bytes 2297864 | tf_op jit(solution)/shard_map/ppermute | solution.py:417
  9.2 4.4 %all-to-all-start.5 = ((f32[16,1,128]{2,1,0:T(1,128)}), f32[16,1,128]{2,1,0:T(1,128)}, u32[]{:S(2)}, u32[]{:S(2)}) async-start(f32[16,1,128]{2,1,0:T(1,128)} %bitcast.29), calls=%async_computation.5 | async-start | bytes 16384 | tf_op jit(solution)/shard_map/all_to_all | solution.py:446
  13.6 0.0 collective-permute-done.19.near_ref.after_at.near_tag_ref
  13.6 0.0 copy-start.12
  13.6 3.2 %pack_grads.3 = (bf16[176,5376]{1,0:T(8,128)(2,1)}, bf16[176,1792]{1,0:T(8,128)(2,1)S(1)}) custom-call(bf16[176,256]{1,0:T(8,128)(2,1)S(1)} %get-tuple-element.107.pick_ref, bf16[256,7168]{1,0:T(8,128)(2,1)} %bitcast.84, bf16[176,2176]{1,0:T(8,128)(2,1)S(1)} %collective-permute-done.19.near_ref.after_at.near_tag_ref), custom_call_target="tpu_custom_call" | custom-call | flops 12918456320 | bytes 7340032 | tf_op jit(solution)/shard_map/pack_grads/pallas_call | solution.py:188
  16.8 5.0 %collective-permute-start.22 = (bf16[176,5376]{1,0:T(8,128)(2,1)}, bf16[176,5376]{1,0:T(8,128)(2,1)}, u32[]{:S(2)}, u32[]{:S(2)}) collective-permute-start(bf16[176,5376]{1,0:T(8,128)(2,1)} %get-tuple-element.109.own_at), channel_id=1, source_target_pairs={{0,56},{4,12},{8,0},{12,20},{16,8},{20,28},{24,16},{28,36},{32,24}... | collective-permute-start | bytes 5677064 | tf_op jit(solution)/shard_map/ppermute | solution.py:417
  21.8 1.9 %collective-permute-start.23 = (bf16[176,5376]{1,0:T(8,128)(2,1)}, bf16[176,5376]{1,0:T(8,128)(2,1)}, u32[]{:S(2)}, u32[]{:S(2)}) collective-permute-start(bf16[176,5376]{1,0:T(8,128)(2,1)} %get-tuple-element.109.own_at), channel_id=1, source_target_pairs={{0,4},{4,0},{8,12},{12,8},{16,20},{20,16},{24,28},{28,24},{32,36},... | collective-permute-start | bytes 5677064 | tf_op jit(solution)/shard_map/ppermute | solution.py:422
  23.7 0.0 collective-permute-done.18.far_ref.far_tag_ref
  23.8 0.0 copy-start.8
  23.8 1.6 %gram.3 = bf16[192,640]{1,0:T(8,128)(2,1)} custom-call(bf16[176,2176]{1,0:T(8,128)(2,1)S(1)} %collective-permute-done.18.far_ref.far_tag_ref, bf16[176,2176]{1,0:T(8,128)(2,1)S(1)} %collective-permute-done.19.near_ref.after_at.near_tag_ref, bf16[176,2176]{1,0:T(8,128)(2,1)S(1)} %get-tuple-element.104.own_ref.own_tag_ref, f32[1,2048]{1,0:T(1,128)S(1)} %copy-done.12, ...), custom_call_target="tpu_custom_call" | custom-call | flops 241591910400 | bytes 2162688 | tf_op jit(solution)/shard_map/gram/pallas_call | solution.py:243
  25.4 0.0 all-to-all-done.5
  25.4 7.3 %all-to-all-start.4 = ((bf16[4,48,640]{2,1,0:T(8,128)(2,1)}), bf16[4,48,640]{2,1,0:T(8,128)(2,1)S(1)}, u32[]{:S(2)}, u32[]{:S(2)}) async-start(bf16[4,48,640]{2,1,0:T(8,128)(2,1)} %bitcast.27), calls=%async_computation.4 | async-start | bytes 491520 | tf_op jit(solution)/shard_map/all_to_all | solution.py:428
  32.6 3.4 %collective-permute-start.20 = (bf16[176,1792]{1,0:T(8,128)(2,1)S(1)}, bf16[176,1792]{1,0:T(8,128)(2,1)}, u32[]{:S(2)}, u32[]{:S(2)}) collective-permute-start(bf16[176,1792]{1,0:T(8,128)(2,1)S(1)} %get-tuple-element.108.own_ref), channel_id=1, source_target_pairs={{0,56},{4,12},{8,0},{12,20},{16,8},{20,28},{24,16},{28,36},{32,24}... | collective-permute-start | bytes 1892360 | tf_op jit(solution)/shard_map/ppermute | solution.py:417
  36.0 1.9 %collective-permute-start.21 = (bf16[176,1792]{1,0:T(8,128)(2,1)S(1)}, bf16[176,1792]{1,0:T(8,128)(2,1)}, u32[]{:S(2)}, u32[]{:S(2)}) collective-permute-start(bf16[176,1792]{1,0:T(8,128)(2,1)S(1)} %get-tuple-element.108.own_ref), channel_id=1, source_target_pairs={{0,4},{4,0},{8,12},{12,8},{16,20},{20,16},{24,28},{28,24},{32,36},... | collective-permute-start | bytes 1892360 | tf_op jit(solution)/shard_map/ppermute | solution.py:422
  37.9 3.9 %all-to-all-done.4.parts_ref = bf16[4,48,640]{2,1,0:T(8,128)(2,1)S(1)} async-done(((bf16[4,48,640]{2,1,0:T(8,128)(2,1)}), bf16[4,48,640]{2,1,0:T(8,128)(2,1)S(1)}, u32[]{:S(2)}, u32[]{:S(2)}) %all-to-all-start.4) | async-done | bytes 245792 | tf_op jit(solution)/shard_map/all_to_all | solution.py:428
  41.8 1.4 %sum_and_spread.3 = (bf16[4,48,640]{2,1,0:T(8,128)(2,1)}, f32[1,128]{1,0:T(1,128)S(1)}) custom-call(bf16[4,48,640]{2,1,0:T(8,128)(2,1)S(1)} %all-to-all-done.4.parts_ref, f32[16,128]{1,0:T(8,128)} %bitcast.30.note_ref), custom_call_target="tpu_custom_call" | custom-call | tf_op jit(solution)/shard_map/sum_and_spread/pallas_call | solution.py:332
  43.2 3.4 %all-to-all-start.6 = ((bf16[4,48,640]{2,1,0:T(8,128)(2,1)}), bf16[4,48,640]{2,1,0:T(8,128)(2,1)S(1)}, u32[]{:S(2)}, u32[]{:S(2)}) async-start(bf16[4,48,640]{2,1,0:T(8,128)(2,1)} %get-tuple-element.110), calls=%async_computation.6 | async-start | bytes 491520 | tf_op jit(solution)/shard_map/all_to_all | solution.py:429
  46.7 3.8 %head_grams.3.head_ref = f32[192,640]{1,0:T(8,128)S(1)} custom-call(bf16[176,5376]{1,0:T(8,128)(2,1)} %collective-permute-done.22.far_at, bf16[176,5376]{1,0:T(8,128)(2,1)} %collective-permute-done.23.near_at, bf16[176,5376]{1,0:T(8,128)(2,1)} %get-tuple-element.109.own_at, f32[1,7168]{1,0:T(1,128)S(1)} %copy-done.8, s32[1]{0:T(128)} %bitcast.26.parity_ref), custom_call_target="tpu_custom_call" | custom-call | flops 2113929216 | bytes 5677056 | tf_op jit(solution)/shard_map/head_grams/pallas_call | solution.py:306
  50.5 0.8 copy-done
  51.3 2.1 %all-to-all-done.6 = bf16[4,48,640]{2,1,0:T(8,128)(2,1)S(1)} async-done(((bf16[4,48,640]{2,1,0:T(8,128)(2,1)}), bf16[4,48,640]{2,1,0:T(8,128)(2,1)S(1)}, u32[]{:S(2)}, u32[]{:S(2)}) %all-to-all-start.6) | async-done | bytes 245792 | tf_op jit(solution)/shard_map/all_to_all | solution.py:429
  53.4 1.0 %copy-done.1 = f32[192,640]{1,0:T(8,128)S(1)} copy-done((f32[192,640]{1,0:T(8,128)S(1)}, f32[192,640]{1,0:T(8,128)}, u32[]{:S(2)}) %copy-start.1) | copy-done | bytes 491544
  54.4 2.8 %finish.3 = f32[32,128]{1,0:T(8,128)S(1)} custom-call(bf16[176,1792]{1,0:T(8,128)(2,1)} %collective-permute-done.20.far_ref, bf16[176,1792]{1,0:T(8,128)(2,1)} %collective-permute-done.21.near_ref, bf16[176,1792]{1,0:T(8,128)(2,1)S(1)} %get-tuple-element.108.own_ref, f32[1,7168]{1,0:T(1,128)S(1)} %copy-done.8, f32[192,640]{1,0:T(8,128)S(1)} %copy-done.1, ...), custom_call_target="tpu_custom_call" | custom-call | tf_op jit(solution)/shard_map/finish/pallas_call | solution.py:391
  57.2 19.2 %all_to_all.54 = f32[32,1,128]{2,1,0:T(1,128)S(1)} all-to-all(f32[32,1,128]{2,1,0:T(1,128)S(1)} %bitcast.75), channel_id=1, replica_groups=mesh['layer'=8,'ex'=16,'width'=4] {'layer','width'}, dimensions={0} | all-to-all | bytes 32768 | tf_op jit(solution)/shard_map/all_to_all | solution.py:454
  76.3 0.1 reduce_sum.45
  76.4 2.8 %collective-permute-start.24 = (f32[128]{0:T(128)S(1)}, f32[128]{0:T(128)S(1)}, u32[]{:S(2)}, u32[]{:S(2)}) collective-permute-start(f32[128]{0:T(128)S(1)} %reduce_sum.45), channel_id=1, source_target_pairs={{0,8},{8,16},{16,24},{24,32},{32,40},{40,48},{48,56},{56,0},{1,9},... | collective-permute-start | bytes 1544 | tf_op jit(solution)/shard_map/ppermute | solution.py:456
  79.2 3.9 %collective-permute-done.24 = f32[128]{0:T(128)S(1)} collective-permute-done((f32[128]{0:T(128)S(1)}, f32[128]{0:T(128)S(1)}, u32[]{:S(2)}, u32[]{:S(2)}) %collective-permute-start.24) | collective-permute-done | bytes 544 | tf_op jit(solution)/shard_map/ppermute | solution.py:456
  83.1 0.2 conditional.2
  83.1 0.1 slice.50
  83.3 0.0 copy-start.16
  83.3 0.6 copy-done.16
  (10 shorter events, 0.0 us)
Async XLA Ops:
  1.9 11.7 %collective-permute-start.19 = (bf16[176,2176]{1,0:T(8,128)(2,1)S(1)}, bf16[176,2176]{1,0:T(8,128)(2,1)S(1)}, u32[]{:S(2)}, u32[]{:S(2)}) collective-permute-start(bf16[176,2176]{1,0:T(8,128)(2,1)S(1)} %get-tuple-element.104.own_ref.own_tag_ref), channel_id=1, source_target_pairs={{0,4},{4,0},{8,12},{12,8},{16,20},{20,16},{24,28},{28,24},{32,36},... | collective-permute-start | bytes 2297864 | tf_op jit(solution)/shard_map/ppermute | solution.py:422
  3.8 20.0 %collective-permute-start.18 = (bf16[176,2176]{1,0:T(8,128)(2,1)S(1)}, bf16[176,2176]{1,0:T(8,128)(2,1)S(1)}, u32[]{:S(2)}, u32[]{:S(2)}) collective-permute-start(bf16[176,2176]{1,0:T(8,128)(2,1)S(1)} %get-tuple-element.104.own_ref.own_tag_ref), channel_id=1, source_target_pairs={{0,56},{4,12},{8,0},{12,20},{16,8},{20,28},{24,16},{28,36},{32,24}... | collective-permute-start | bytes 2297864 | tf_op jit(solution)/shard_map/ppermute | solution.py:417
  9.2 16.2 %all-to-all-start.5 = ((f32[16,1,128]{2,1,0:T(1,128)}), f32[16,1,128]{2,1,0:T(1,128)}, u32[]{:S(2)}, u32[]{:S(2)}) async-start(f32[16,1,128]{2,1,0:T(1,128)} %bitcast.29), calls=%async_computation.5 | async-start | bytes 16384 | tf_op jit(solution)/shard_map/all_to_all | solution.py:446
  13.6 10.2 %copy-start.12 = (f32[1,2048]{1,0:T(1,128)S(1)}, f32[1,2048]{1,0:T(1,128)}, u32[]{:S(2)}) copy-start(f32[1,2048]{1,0:T(1,128)} %scale_ref.3) | copy-start | bytes 24580
  16.8 29.8 %collective-permute-start.22 = (bf16[176,5376]{1,0:T(8,128)(2,1)}, bf16[176,5376]{1,0:T(8,128)(2,1)}, u32[]{:S(2)}, u32[]{:S(2)}) collective-permute-start(bf16[176,5376]{1,0:T(8,128)(2,1)} %get-tuple-element.109.own_at), channel_id=1, source_target_pairs={{0,56},{4,12},{8,0},{12,20},{16,8},{20,28},{24,16},{28,36},{32,24}... | collective-permute-start | bytes 5677064 | tf_op jit(solution)/shard_map/ppermute | solution.py:417
  21.8 24.8 %collective-permute-start.23 = (bf16[176,5376]{1,0:T(8,128)(2,1)}, bf16[176,5376]{1,0:T(8,128)(2,1)}, u32[]{:S(2)}, u32[]{:S(2)}) collective-permute-start(bf16[176,5376]{1,0:T(8,128)(2,1)} %get-tuple-element.109.own_at), channel_id=1, source_target_pairs={{0,4},{4,0},{8,12},{12,8},{16,20},{20,16},{24,28},{28,24},{32,36},... | collective-permute-start | bytes 5677064 | tf_op jit(solution)/shard_map/ppermute | solution.py:422
  23.8 22.9 %copy-start.8 = (f32[1,7168]{1,0:T(1,128)S(1)}, f32[1,7168]{1,0:T(1,128)}, u32[]{:S(2)}) copy-start(f32[1,7168]{1,0:T(1,128)} %scale_ref.5) | copy-start | bytes 86020
  25.4 16.4 %all-to-all-start.4 = ((bf16[4,48,640]{2,1,0:T(8,128)(2,1)}), bf16[4,48,640]{2,1,0:T(8,128)(2,1)S(1)}, u32[]{:S(2)}, u32[]{:S(2)}) async-start(bf16[4,48,640]{2,1,0:T(8,128)(2,1)} %bitcast.27), calls=%async_computation.4 | async-start | bytes 491520 | tf_op jit(solution)/shard_map/all_to_all | solution.py:428
  32.6 18.7 %collective-permute-start.20 = (bf16[176,1792]{1,0:T(8,128)(2,1)S(1)}, bf16[176,1792]{1,0:T(8,128)(2,1)}, u32[]{:S(2)}, u32[]{:S(2)}) collective-permute-start(bf16[176,1792]{1,0:T(8,128)(2,1)S(1)} %get-tuple-element.108.own_ref), channel_id=1, source_target_pairs={{0,56},{4,12},{8,0},{12,20},{16,8},{20,28},{24,16},{28,36},{32,24}... | collective-permute-start | bytes 1892360 | tf_op jit(solution)/shard_map/ppermute | solution.py:417
  36.0 15.3 %collective-permute-start.21 = (bf16[176,1792]{1,0:T(8,128)(2,1)S(1)}, bf16[176,1792]{1,0:T(8,128)(2,1)}, u32[]{:S(2)}, u32[]{:S(2)}) collective-permute-start(bf16[176,1792]{1,0:T(8,128)(2,1)S(1)} %get-tuple-element.108.own_ref), channel_id=1, source_target_pairs={{0,4},{4,0},{8,12},{12,8},{16,20},{20,16},{24,28},{28,24},{32,36},... | collective-permute-start | bytes 1892360 | tf_op jit(solution)/shard_map/ppermute | solution.py:422
  43.2 10.2 %all-to-all-start.6 = ((bf16[4,48,640]{2,1,0:T(8,128)(2,1)}), bf16[4,48,640]{2,1,0:T(8,128)(2,1)S(1)}, u32[]{:S(2)}, u32[]{:S(2)}) async-start(bf16[4,48,640]{2,1,0:T(8,128)(2,1)} %get-tuple-element.110), calls=%async_computation.6 | async-start | bytes 491520 | tf_op jit(solution)/shard_map/all_to_all | solution.py:429
  50.5 0.8 copy-start
  53.4 1.0 %copy-start.1 = (f32[192,640]{1,0:T(8,128)S(1)}, f32[192,640]{1,0:T(8,128)}, u32[]{:S(2)}) copy-start(f32[192,640]{1,0:T(8,128)} %copy-done) | copy-start | bytes 1474564
  76.4 6.7 %collective-permute-start.24 = (f32[128]{0:T(128)S(1)}, f32[128]{0:T(128)S(1)}, u32[]{:S(2)}, u32[]{:S(2)}) collective-permute-start(f32[128]{0:T(128)S(1)} %reduce_sum.45), channel_id=1, source_target_pairs={{0,8},{8,16},{16,24},{24,32},{32,40},{40,48},{48,56},{56,0},{1,9},... | collective-permute-start | bytes 1544 | tf_op jit(solution)/shard_map/ppermute | solution.py:456
  83.3 0.6 copy-start.16
